TPU v7x, 128 devices: a whole 4x4x4 slice. The times are simulated.
128 devices in a mesh: grp: 4 (over y), dev: 32 (over z, x, core).
Axes of the slice: x: 4, y: 4, z: 4, core: 2. Of those that a mesh axis runs over, the one named last changes fastest.
Arguments:
- points: float32 [64, 196608], P(None, 'dev'), may hold values from -6 to 6
- weights: float32 [196608, 128], P('dev'), may hold values from -4 to 4
- proj: float32 [256, 196608], P(None, 'dev'), may hold values from -0.078125 to 0.078125
- fetch_table: int32 [3, 32, 32, 2], P(None, 'dev'), may hold values from 0 to 11, as said below
- near_list: int32 [384, 16], P('dev'), may hold values from 0 to 63, as said below
- far_list: int32 [384, 8], P('dev'), may hold values from 0 to 31, as said below
- skel_idx: int32 [32, 256], P('dev'), may hold values from 0 to 6143, as said below
Outputs:
- potential: float32 [196608, 128], P('dev')
Inputs may be any that keep to these rules, and one draw needn't show every extreme that they name: Entries of fetch_table[r, d, e] are distinct local leaf numbers of column e. `near_list`: the 16 slots of one target leaf are distinct. `far_list`: the 8 nodes of one target leaf are distinct, and one of them is node (c + 1) mod 32 for the leaf's column c. `skel_idx`: the 256 skeleton points of one node are distinct.
All inputs are finite; a program needn't handle non-finite values.
Results may differ from a plain program's by a relative error of at most 0.0003.
Values sent between devices are 32-bit elements; how exact they have to be, the bound alone decides.
A program may use at most 192 MiB of HBM per device.

v0:
```python
import jax
import jax.numpy as jnp
from jax import lax
from jax.sharding import PartitionSpec as P


def kernel_sum(target, sources, values):
    high = lax.Precision.HIGHEST
    inner = jnp.einsum("dt,jds->tjs", target, sources, precision=high)
    target_norm = jnp.sum(target * target, axis=0)
    source_norm = jnp.sum(sources * sources, axis=1)
    distance = target_norm[:, None, None] + source_norm[None] - 2.0 * inner
    kernel = jnp.exp(-distance * (2.0 / target.shape[0]))
    return jnp.einsum("tjs,jsw->tw", kernel, values, precision=high)


def on_device(points, weights, proj, fetch_table, near_list, far_list, skel_idx):
    features, column_points = points.shape
    columns = weights.shape[1]
    devices = lax.axis_size("dev")
    groups = lax.axis_size("grp")
    targets = near_list.shape[0]
    leaf_size = column_points // targets
    row_leaves = targets // (groups - 1)
    capacity = fetch_table.shape[3]
    skeleton = skel_idx.shape[1]
    group_index = lax.axis_index("grp")
    near_row = jnp.minimum(group_index, groups - 2)
    far_side = group_index == groups - 1
    leaf_coords = points.reshape(features, targets, leaf_size)
    leaf_weights = weights.reshape(targets, leaf_size, columns)
    requests = lax.dynamic_index_in_dim(fetch_table[:, 0], near_row, 0, keepdims=False)
    asked = lax.all_to_all(requests, "dev", split_axis=0, concat_axis=0, tiled=True)
    coords = jnp.moveaxis(jnp.take(leaf_coords, asked, axis=1), 0, 2)
    values = jnp.take(leaf_weights, asked, axis=0)
    fetched_coords = lax.all_to_all(coords, "dev", split_axis=0, concat_axis=0, tiled=True)
    fetched_values = lax.all_to_all(values, "dev", split_axis=0, concat_axis=0, tiled=True)
    flat_coords = fetched_coords.reshape(devices * capacity, features, leaf_size)
    flat_values = fetched_values.reshape(devices * capacity, leaf_size, columns)
    local_skeleton = jnp.take(points, skel_idx[0], axis=1)
    share_len = column_points // groups
    share_start = group_index * share_len
    share_proj = lax.dynamic_slice_in_dim(proj, share_start, share_len, 1)
    share_weights = lax.dynamic_slice_in_dim(weights, share_start, share_len, 0)
    partial_value = jnp.dot(
        share_proj,
        share_weights,
        preferred_element_type=jnp.float32,
        precision=lax.Precision.HIGHEST,
    )
    node_index = lax.axis_index("dev")
    owner_mask = jnp.where(far_side, 1.0, 0.0).astype(jnp.float32)
    table_coords = jnp.zeros((devices, features, skeleton), jnp.float32)
    table_coords = lax.dynamic_update_index_in_dim(
        table_coords, local_skeleton * owner_mask, node_index, 0
    )
    table_weights = jnp.zeros((devices, skeleton, columns), jnp.float32)
    table_weights = lax.dynamic_update_index_in_dim(table_weights, partial_value, node_index, 0)
    skel_coords, skel_weights = lax.psum((table_coords, table_weights), ("grp", "dev"))

    def near_work():
        slots = lax.dynamic_slice_in_dim(near_list, near_row * row_leaves, row_leaves, 0)
        leaf_numbers = near_row * row_leaves + jnp.arange(row_leaves, dtype=jnp.int32)

        def near_leaf(items):
            leaf_number, leaf_slots = items
            target = jnp.take(leaf_coords, leaf_number, axis=1)
            return kernel_sum(
                target,
                jnp.take(flat_coords, leaf_slots, axis=0),
                jnp.take(flat_values, leaf_slots, axis=0),
            )

        block = lax.map(near_leaf, (leaf_numbers, slots))
        empty = jnp.zeros((targets, leaf_size, columns), jnp.float32)
        return lax.dynamic_update_slice_in_dim(empty, block, near_row * row_leaves, 0)

    def far_work():

        def far_leaf(items):
            leaf_number, node_ids = items
            target = jnp.take(leaf_coords, leaf_number, axis=1)
            return kernel_sum(
                target,
                jnp.take(skel_coords, node_ids, axis=0),
                jnp.take(skel_weights, node_ids, axis=0),
            )

        return lax.map(far_leaf, (jnp.arange(targets, dtype=jnp.int32), far_list))

    contribution = lax.cond(far_side, far_work, near_work)
    total = lax.psum(contribution, "grp")
    return total.reshape(column_points, columns)


def solution(mesh):
    placed = (
        P(None, "dev"),
        P("dev", None),
        P(None, "dev"),
        P(None, "dev", None, None),
        P("dev", None),
        P("dev", None),
        P("dev", None),
    )
    return jax.shard_map(
        on_device, mesh=mesh, in_specs=placed, out_specs=P("dev", None), check_vma=False
    )
```

profile of v0, /device:TPU:0, one launch (start us, length us, event | category | flops | bytes accessed | tf_op | source)
XLA Modules:
  0.0 819.6 jit_solution(13350892789192930071)
XLA Ops:
  8.1 8.2 %all-to-all-start = ((s32[32,1,2]{2,1,0:T(1,128)}), s32[32,1,2]{2,1,0:T(1,128)S(1)}, u32[]{:S(2)}, u32[]{:S(2)}) async-start(s32[32,1,2]{2,1,0:T(1,128)} %copy.36), calls=%async_computation | async-start | bytes 32768 | tf_op jit(solution)/shard_map/all_to_all | solution.py:33
  19.0 4.6 all-to-all-done
  24.1 5.7 gather_fusion.4
  29.8 8.5 %broadcast_select_fusion.1 = f32[32,2,64,512]{3,2,1,0:T(8,128)} fusion(f32[32,2,64,512]{3,2,1,0:T(8,128)} %bitcast.103, pred[32,2]{1,0:T(8,128)(4,1)S(1)} %copy.38), kind=kLoop, calls=%fused_computation.87 | loop fusion | flops 2097152 | bytes 16777280 | tf_op jit(solution)/shard_map/jit(_take)/select_n | solution.py:34
  38.3 5.0 all-to-all-start.1
  43.3 7.4 gather_fusion.5
  50.6 11.6 %broadcast_select_fusion = f32[32,2,512,128]{3,2,1,0:T(8,128)} fusion(f32[32,2,512,128]{3,2,1,0:T(8,128)} %bitcast.101, pred[32,2]{1,0:T(8,128)(4,1)S(1)} %copy.38), kind=kLoop, calls=%fused_computation.86 | loop fusion | flops 4194304 | bytes 33554496 | tf_op jit(solution)/shard_map/jit(_take)/select_n | solution.py:35
  62.2 86.9 %all-to-all-done.1 = f32[32,2,64,512]{3,2,1,0:T(8,128)} async-done(((f32[32,2,64,512]{3,2,1,0:T(8,128)}), f32[32,2,64,512]{3,2,1,0:T(8,128)}, u32[]{:S(2)}, u32[]{:S(2)}) %all-to-all-start.1) | async-done | bytes 8388640 | tf_op jit(solution)/shard_map/all_to_all | solution.py:36
  149.1 5.2 all-to-all-start.2
  154.4 3.3 copy.43
  162.8 3.5 fusion.75
  170.4 311.0 %all-reduce.6.cloned.1.call-done = (f32[32,64,256]{2,1,0:T(8,128)}, f32[32,256,128]{2,1,0:T(8,128)}) async-done(((f32[32,64,256]{2,1,0:T(8,128)}, f32[32,256,128]{2,1,0:T(8,128)}), (f32[32,64,256]{2,1,0:T(8,128)}, f32[32,256,128]{2,1,0:T(8,128)})) %all-reduce.6.cloned.1.call-update) | async-done | bytes 6291472 | tf_op jit(solution)/shard_map/psum | solution.py:59
  481.4 223.2 %conditional.1 = (f32[12,512,128]{2,1,0:T(8,128)}) conditional(s32[]{:T(128)} %convert_element_type.3, (s32[]{:T(128)}, s32[12,16]{1,0:T(8,128)}, f32[32,2,64,512]{3,2,1,0:T(8,128)}, f32[32,2,512,128]{3,2,1,0:T(8,128)}, f32[64,12,512]{2,1,0:T(8,128)}) %tuple.20, (f32[64,12,512]{2,1,0:T(8,128)}, s32[12,8]{0,1:T(8,128)S(1)}, f32[32,64,256]{2,1,0:T(8,128)}, ...), branch_computations={%region_2.0_spmd, %region_7.13_spmd} | conditional | flops 9687917568 | bytes 60630836 | solution.py:91
  482.1 218.3 %while.19 = (s32[]{:T(128)}, f32[4,512,128]{2,1,0:T(8,128)}, s32[4]{0:T(128)S(1)}, f32[64,12,512]{2,1,0:T(8,128)}, s32[4,16]{1,0:T(4,128)S(1)}, /*index=5*/f32[6...) while((s32[]{:T(128)}, f32[4,512,128]{2,1,0:T(8,128)}, ...), condition=%wide.region_6.7_spmd, body=%wide.region_3.6_spmd.sunk | while | flops 9687917568 | bytes 55387260 | solution.py:74
  486.0 4.1 gather_fusion.3
  490.0 16.2 %fusion.112 = f32[512,16,512]{2,0,1:T(8,128)} fusion(f32[16,64,512]{2,1,0:T(8,128)S(1)} %gather_fusion.3, pred[16]{0:T(512)(128)(4,1)S(1)} %compare_and_fusion.7, f32[64,1,512]{2,1,0:T(1,128)S(1)} %constant_dynamic-slice_fusion.9, pred[]{:T(512)S(6)} %and.57), kind=kOutput, calls=%fused_computation.22.clone.1 | convolution fusion | flops 3221782528 | bytes 19005456 | tf_op jit(solution)/shard_map/cond/branch_0_fun/while/body/eval_jaxpr/dt,jds->tjs/dot_general | solution.py:9
  506.6 8.5 %gather_fusion.2 = f32[16,512,128]{2,1,0:T(8,128)} fusion(f32[64,512,128]{2,1,0:T(8,128)} %get-tuple-element.330, s32[1024]{0:T(1024)S(1)} %pad_clamp_fusion.7), kind=kCustom, calls=%fused_computation.1.clone.1 | custom fusion | bytes 8388672 | tf_op jit(solution)/shard_map/cond/branch_0_fun/while/body/eval_jaxpr/jit(_take)/gather | solution.py:71
  515.1 21.5 %fusion.114 = f32[4,512,128]{2,1,0:T(8,128)} fusion(f32[4,512,128]{2,1,0:T(8,128)} %get-tuple-element.314, s32[]{:T(128)} %get-tuple-element.313, f32[16,512,128]{2,1,0:T(8,128)} %gather_fusion.2, pred[16]{0:T(512)(128)(4,1)S(1)} %compare_and_fusion.7, f32[512,16,512]{2,0,1:T(8,128)} %fusion.112, f32[16,512]{1,0:T(8,128)S(1)} %multiply_reduce_fusion.5, ...), kind=kOutput, calls=%fused_computation.25.clone.1 | convolution fusion | flops 6464471040 | bytes 21269008 | tf_op jit(solution)/shard_map/cond/branch_0_fun/while/body/eval_jaxpr/tjs,jsw->tw/dot_general | solution.py:14
  540.5 4.1 gather_fusion.3
  544.6 16.2 %fusion.112 = f32[512,16,512]{2,0,1:T(8,128)} fusion(f32[16,64,512]{2,1,0:T(8,128)S(1)} %gather_fusion.3, pred[16]{0:T(512)(128)(4,1)S(1)} %compare_and_fusion.7, f32[64,1,512]{2,1,0:T(1,128)S(1)} %constant_dynamic-slice_fusion.9, pred[]{:T(512)S(6)} %and.57), kind=kOutput, calls=%fused_computation.22.clone.1 | convolution fusion | flops 3221782528 | bytes 19005456 | tf_op jit(solution)/shard_map/cond/branch_0_fun/while/body/eval_jaxpr/dt,jds->tjs/dot_general | solution.py:9
  561.2 8.5 %gather_fusion.2 = f32[16,512,128]{2,1,0:T(8,128)} fusion(f32[64,512,128]{2,1,0:T(8,128)} %get-tuple-element.330, s32[1024]{0:T(1024)S(1)} %pad_clamp_fusion.7), kind=kCustom, calls=%fused_computation.1.clone.1 | custom fusion | bytes 8388672 | tf_op jit(solution)/shard_map/cond/branch_0_fun/while/body/eval_jaxpr/jit(_take)/gather | solution.py:71
  569.7 21.5 %fusion.114 = f32[4,512,128]{2,1,0:T(8,128)} fusion(f32[4,512,128]{2,1,0:T(8,128)} %get-tuple-element.314, s32[]{:T(128)} %get-tuple-element.313, f32[16,512,128]{2,1,0:T(8,128)} %gather_fusion.2, pred[16]{0:T(512)(128)(4,1)S(1)} %compare_and_fusion.7, f32[512,16,512]{2,0,1:T(8,128)} %fusion.112, f32[16,512]{1,0:T(8,128)S(1)} %multiply_reduce_fusion.5, ...), kind=kOutput, calls=%fused_computation.25.clone.1 | convolution fusion | flops 6464471040 | bytes 21269008 | tf_op jit(solution)/shard_map/cond/branch_0_fun/while/body/eval_jaxpr/tjs,jsw->tw/dot_general | solution.py:14
  595.1 4.1 gather_fusion.3
  599.2 16.2 %fusion.112 = f32[512,16,512]{2,0,1:T(8,128)} fusion(f32[16,64,512]{2,1,0:T(8,128)S(1)} %gather_fusion.3, pred[16]{0:T(512)(128)(4,1)S(1)} %compare_and_fusion.7, f32[64,1,512]{2,1,0:T(1,128)S(1)} %constant_dynamic-slice_fusion.9, pred[]{:T(512)S(6)} %and.57), kind=kOutput, calls=%fused_computation.22.clone.1 | convolution fusion | flops 3221782528 | bytes 19005456 | tf_op jit(solution)/shard_map/cond/branch_0_fun/while/body/eval_jaxpr/dt,jds->tjs/dot_general | solution.py:9
  615.8 8.5 %gather_fusion.2 = f32[16,512,128]{2,1,0:T(8,128)} fusion(f32[64,512,128]{2,1,0:T(8,128)} %get-tuple-element.330, s32[1024]{0:T(1024)S(1)} %pad_clamp_fusion.7), kind=kCustom, calls=%fused_computation.1.clone.1 | custom fusion | bytes 8388672 | tf_op jit(solution)/shard_map/cond/branch_0_fun/while/body/eval_jaxpr/jit(_take)/gather | solution.py:71
  624.3 21.5 %fusion.114 = f32[4,512,128]{2,1,0:T(8,128)} fusion(f32[4,512,128]{2,1,0:T(8,128)} %get-tuple-element.314, s32[]{:T(128)} %get-tuple-element.313, f32[16,512,128]{2,1,0:T(8,128)} %gather_fusion.2, pred[16]{0:T(512)(128)(4,1)S(1)} %compare_and_fusion.7, f32[512,16,512]{2,0,1:T(8,128)} %fusion.112, f32[16,512]{1,0:T(8,128)S(1)} %multiply_reduce_fusion.5, ...), kind=kOutput, calls=%fused_computation.25.clone.1 | convolution fusion | flops 6464471040 | bytes 21269008 | tf_op jit(solution)/shard_map/cond/branch_0_fun/while/body/eval_jaxpr/tjs,jsw->tw/dot_general | solution.py:14
  649.7 4.1 gather_fusion.3
  653.8 16.2 %fusion.112 = f32[512,16,512]{2,0,1:T(8,128)} fusion(f32[16,64,512]{2,1,0:T(8,128)S(1)} %gather_fusion.3, pred[16]{0:T(512)(128)(4,1)S(1)} %compare_and_fusion.7, f32[64,1,512]{2,1,0:T(1,128)S(1)} %constant_dynamic-slice_fusion.9, pred[]{:T(512)S(6)} %and.57), kind=kOutput, calls=%fused_computation.22.clone.1 | convolution fusion | flops 3221782528 | bytes 19005456 | tf_op jit(solution)/shard_map/cond/branch_0_fun/while/body/eval_jaxpr/dt,jds->tjs/dot_general | solution.py:9
  670.3 8.5 %gather_fusion.2 = f32[16,512,128]{2,1,0:T(8,128)} fusion(f32[64,512,128]{2,1,0:T(8,128)} %get-tuple-element.330, s32[1024]{0:T(1024)S(1)} %pad_clamp_fusion.7), kind=kCustom, calls=%fused_computation.1.clone.1 | custom fusion | bytes 8388672 | tf_op jit(solution)/shard_map/cond/branch_0_fun/while/body/eval_jaxpr/jit(_take)/gather | solution.py:71
  678.8 21.5 %fusion.114 = f32[4,512,128]{2,1,0:T(8,128)} fusion(f32[4,512,128]{2,1,0:T(8,128)} %get-tuple-element.314, s32[]{:T(128)} %get-tuple-element.313, f32[16,512,128]{2,1,0:T(8,128)} %gather_fusion.2, pred[16]{0:T(512)(128)(4,1)S(1)} %compare_and_fusion.7, f32[512,16,512]{2,0,1:T(8,128)} %fusion.112, f32[16,512]{1,0:T(8,128)S(1)} %multiply_reduce_fusion.5, ...), kind=kOutput, calls=%fused_computation.25.clone.1 | convolution fusion | flops 6464471040 | bytes 21269008 | tf_op jit(solution)/shard_map/cond/branch_0_fun/while/body/eval_jaxpr/tjs,jsw->tw/dot_general | solution.py:14
  704.6 104.4 %all-reduce.4.cloned.1.call-done = f32[6144,128]{1,0:T(8,128)} async-done(((f32[6144,128]{1,0:T(8,128)}), f32[6144,128]{1,0:T(8,128)}) %all-reduce.4.cloned.1.call-update) | async-done | bytes 3145744 | tf_op jit(solution)/shard_map/psum | solution.py:92
  809.0 3.8 copy.95
  (67 shorter events, 28.4 us)
Async XLA Ops:
  6.5 36.7 %copy-start = (f32[6144,128]{1,0:T(8,128)S(1)}, f32[6144,128]{1,0:T(8,128)}, u32[]{:S(2)}) copy-start(f32[6144,128]{1,0:T(8,128)} %param.16) | copy-start | bytes 9437188
  8.1 15.6 %all-to-all-start = ((s32[32,1,2]{2,1,0:T(1,128)}), s32[32,1,2]{2,1,0:T(1,128)S(1)}, u32[]{:S(2)}, u32[]{:S(2)}) async-start(s32[32,1,2]{2,1,0:T(1,128)} %copy.36), calls=%async_computation | async-start | bytes 32768 | tf_op jit(solution)/shard_map/all_to_all | solution.py:33
  38.3 110.8 %all-to-all-start.1 = ((f32[32,2,64,512]{3,2,1,0:T(8,128)}), f32[32,2,64,512]{3,2,1,0:T(8,128)}, u32[]{:S(2)}, u32[]{:S(2)}) async-start(f32[32,2,64,512]{3,2,1,0:T(8,128)} %broadcast_select_fusion.1), calls=%async_computation.1 | async-start | bytes 16777216 | tf_op jit(solution)/shard_map/all_to_all | solution.py:36
  149.1 332.3 %all-to-all-start.2 = ((f32[32,2,512,128]{3,2,1,0:T(8,128)}), f32[32,2,512,128]{3,2,1,0:T(8,128)}, u32[]{:S(2)}, u32[]{:S(2)}) async-start(f32[32,2,512,128]{3,2,1,0:T(8,128)} %broadcast_select_fusion), calls=%async_computation.2 | async-start | bytes 33554432 | tf_op jit(solution)/shard_map/all_to_all | solution.py:37
  154.3 3.3 copy-start.4
  154.3 327.1 %all-reduce.6.cloned.1.call-start = ((), (), s32[]{:S(2)}) async-start(), calls=%async_computation.4 | async-start | bytes 12582912 | tf_op jit(solution)/shard_map/psum | solution.py:59
  166.2 2.3 copy-start.2
  168.4 312.9 %copy-start.3 = (s32[12,8]{0,1:T(8,128)S(1)}, s32[12,8]{0,1:T(8,128)}, u32[]{:S(2)}) copy-start(s32[12,8]{0,1:T(8,128)} %param.20) | copy-start | bytes 1156
  168.5 640.5 %all-reduce.4.cloned.1.call-start = ((), (), s32[]{:S(2)}) async-start(), calls=%async_computation.3 | async-start | bytes 6291456 | tf_op jit(solution)/shard_map/psum | solution.py:92
  704.6 108.1 %copy-start.1 = (f32[6144,128]{1,0:T(8,128)S(1)}, f32[6144,128]{1,0:T(8,128)}, u32[]{:S(2)}) copy-start(f32[6144,128]{1,0:T(8,128)} %param.16) | copy-start | bytes 9437188
Sparse Core Ops, SparseCore 0:
  168.6 312.7 all-reduce.5
  704.8 104.1 all-reduce.3
where the time goes:
time: 823 us; the launch traced here: 820 us
  waiting for transfers between devices  507 us (62%)
  matrix products  154 us (19%)
  local copies, waits for them, and re-layouts  96.2 us (12%)
  other arithmetic  22.5 us (3%)
  starting transfers between devices  18.5 us (2%)
  between operations  13.5 us (2%)
    psum x1, waiting for transfers between devices, on_device(): lax.psum((table_coords, table_weights), ('grp', 'dev'))  311 us
    psum x1, waiting for transfers between devices, on_device(): total = lax.psum(contribution, 'grp')  104 us
    all_to_all x1, waiting for transfers between devices, on_device(): lax.all_to_all(coords, 'dev', split_axis=0, concat_axis=0, tiled=True)  86.9 us
    dot_general x4, matrix products, kernel_sum(): return jnp.einsum('tjs,jsw->tw', kernel, values, precision=high)  86.1 us
    dot_general x4, matrix products, kernel_sum(): inner = jnp.einsum('dt,jds->tjs', target, sources, precision=high)  64.7 us
    gather x4, local copies, waits for them, and re-layouts, near_leaf(): jnp.take(flat_values, leaf_slots, axis=0)  34 us
  transfers between devices with their start and end apart: 5, of which 4 were waited for; matrix products, arithmetic and copies ran while one was open for 5% of the time, Pallas kernels for 0%

commit v1 on v0

v1 whole, which is shorter than its diff:
```python
import functools
import math

import jax
import jax.numpy as jnp
from jax import lax
from jax.experimental import pallas as pl
from jax.experimental.pallas import tpu as pltpu
from jax.sharding import PartitionSpec as P

F32, BF16 = jnp.float32, jnp.bfloat16
MESH = pl.DeviceIdType.MESH
VMEM = pltpu.VMEM
LOG2E = math.log2(math.e)
SIDE = 4
SPOTS = SIDE * SIDE
LEAF, DIM, WCOL, SKEL = 512, 64, 128, 256
LEAVES = 12
MINE = 3
COLPTS = LEAVES * LEAF
HALF = LEAF // 2
PAYLOAD = MINE * HALF + 8
TARGETS = SPOTS * MINE
SOURCES = 2 * COLPTS + 2 * SKEL
CHUNK = 1024
CUTS = (0, 192, 384, 576, PAYLOAD)


def mm(a, b):
    return jnp.dot(a, b, preferred_element_type=F32)


def split2(v):
    high = v.astype(BF16)
    return high, (v - high.astype(F32)).astype(BF16)


def prepare_kernel(y_ref, points, weights, proj, index, own, table, payload, coords, values):
    step = pl.program_id(0)
    wh, wl = split2(weights[...])
    ph, plow = split2(proj[...])
    value = mm(ph, wh) + mm(ph, wl) + mm(plow, wh)
    rows = lax.broadcasted_iota(jnp.int32, (CHUNK, SKEL), 0) + step * CHUNK
    pick = jnp.where(rows == index[...], 1.0, 0.0).astype(BF16)
    first = points[...].astype(BF16)
    rest = points[...] - first.astype(F32)
    second, third = split2(rest)
    coord = mm(first, pick) + mm(second, pick) + mm(third, pick)

    @pl.when(step == 0)
    def _():
        values[...] = value
        coords[...] = coord
        payload[pl.ds(MINE * HALF, 8), :] = table[...]
        for leaf in range(MINE):
            block = own[:, leaf * LEAF : (leaf + 1) * LEAF]
            packed = jnp.concatenate([block[:, :HALF], block[:, HALF:]], axis=0)
            payload[pl.ds(leaf * HALF, HALF), :] = packed.T

    @pl.when(step > 0)
    def _():
        values[...] += value
        coords[...] += coord


def prepare(y, points, weights, proj, index, table):
    steps = COLPTS // CHUNK
    return pl.pallas_call(
        prepare_kernel,
        out_shape=(
            jax.ShapeDtypeStruct((PAYLOAD, 128), F32),
            jax.ShapeDtypeStruct((DIM, SKEL), F32),
            jax.ShapeDtypeStruct((SKEL, WCOL), F32),
        ),
        grid_spec=pltpu.PrefetchScalarGridSpec(
            num_scalar_prefetch=1,
            grid=(steps,),
            in_specs=[
                pl.BlockSpec((DIM, CHUNK), lambda i, y: (0, i)),
                pl.BlockSpec((CHUNK, WCOL), lambda i, y: (i, 0)),
                pl.BlockSpec((SKEL, CHUNK), lambda i, y: (0, i)),
                pl.BlockSpec((1, SKEL), lambda i, y: (0, 0)),
                pl.BlockSpec((DIM, MINE * LEAF), lambda i, y: (0, y[0])),
                pl.BlockSpec((8, 128), lambda i, y: (0, 0)),
            ],
            out_specs=[
                pl.BlockSpec((PAYLOAD, 128), lambda i, y: (0, 0)),
                pl.BlockSpec((DIM, SKEL), lambda i, y: (0, 0)),
                pl.BlockSpec((SKEL, WCOL), lambda i, y: (0, 0)),
            ],
        ),
        compiler_params=pltpu.CompilerParams(vmem_limit_bytes=32 << 20),
    )(y, points, weights, proj, index, points, table)


def place():
    y, dev = lax.axis_index("grp"), lax.axis_index("dev")
    return y, dev // 8, (dev // 2) % SIDE, dev % 2


def device(y, z, x, core):
    return (y, (z * SIDE + x) * 2 + core)


def stream_axes(k):
    return k < 2, 1 if k % 2 == 0 else SIDE - 1


def moved(k, z, x, first, second):
    x_first, sign = stream_axes(k)
    along_x, along_z = (first, second) if x_first else (second, first)
    return (z + sign * along_z) % SIDE, (x + sign * along_x) % SIDE


def greet(peers):
    barrier = pltpu.get_barrier_semaphore()
    for peer in peers:
        pl.semaphore_signal(barrier, inc=1, device_id=peer, device_id_type=MESH)
    pl.semaphore_wait(barrier, len(peers))


def gather_kernel(
    payload, points, weights, coords, values,
    gathered, points2, weights2, coords2, values2,
    send, recv, pair_send, pair_recv, own_sem,
):
    y, z, x, core = place()
    near = [(1, 0), (SIDE - 1, 0), (0, 1), (0, SIDE - 1)]
    peers = [device(y, (z + a) % SIDE, (x + b) % SIDE, core) for a, b in near]
    sibling = device(y, z, x, 1 - core)
    greet(peers + [sibling])

    def copy(k, i, j, first):
        az, ax = moved(k, z, x, -i, -j)
        spot = az * SIDE + ax
        rows = pl.ds(CUTS[k], CUTS[k + 1] - CUTS[k])
        tz, tx = moved(k, z, x, 1 if first else 0, 0 if first else 1)
        arrival = (i + 1) * SIDE + j if first else i * SIDE + j + 1
        number = i if first else SIDE - 1 + i * (SIDE - 1) + j
        source = payload.at[rows] if i == 0 and j == 0 else gathered.at[spot, rows]
        return pltpu.make_async_remote_copy(
            src_ref=source,
            dst_ref=gathered.at[spot, rows],
            send_sem=send.at[k, number],
            recv_sem=recv.at[k, arrival],
            device_id=device(y, tz, tx, core),
            device_id_type=MESH,
        )

    def wait_arrival(k, i, j):
        az, ax = moved(k, z, x, -i, -j)
        spot = az * SIDE + ax
        rows = pl.ds(CUTS[k], CUTS[k + 1] - CUTS[k])
        pltpu.make_async_copy(gathered.at[spot, rows], gathered.at[spot, rows], recv.at[k, i * SIDE + j]).wait()

    own = pltpu.make_async_copy(payload, gathered.at[z * SIDE + x], own_sem)
    own.start()
    started = []
    for level in range(2 * SIDE - 1):
        for i in range(SIDE):
            j = level - i
            if not 0 <= j < SIDE:
                continue
            for k in range(4):
                if level > 0:
                    wait_arrival(k, i, j)
                if j == 0 and i < SIDE - 1:
                    c = copy(k, i, j, True)
                    c.start()
                    started.append(c)
                if j < SIDE - 1:
                    c = copy(k, i, j, False)
                    c.start()
                    started.append(c)
        if level == 0:
            swaps = []
            for n, (a, b) in enumerate(
                ((points, points2), (weights, weights2), (coords, coords2), (values, values2))
            ):
                c = pltpu.make_async_remote_copy(
                    src_ref=a, dst_ref=b, send_sem=pair_send.at[n], recv_sem=pair_recv.at[n],
                    device_id=sibling, device_id_type=MESH,
                )
                c.start()
                swaps.append(c)
    for c in started:
        c.wait_send()
    for c in swaps:
        c.wait()
    own.wait()


def gather(payload, points, weights, coords, values):
    anywhere = pl.BlockSpec(memory_space=pl.ANY)
    return pl.pallas_call(
        gather_kernel,
        out_shape=(
            jax.ShapeDtypeStruct((SPOTS, PAYLOAD, 128), F32),
            jax.ShapeDtypeStruct(points.shape, F32),
            jax.ShapeDtypeStruct(weights.shape, F32),
            jax.ShapeDtypeStruct(coords.shape, F32),
            jax.ShapeDtypeStruct(values.shape, F32),
        ),
        in_specs=[anywhere] * 5,
        out_specs=[anywhere] * 5,
        scratch_shapes=[
            pltpu.SemaphoreType.DMA((4, 15)),
            pltpu.SemaphoreType.DMA((4, 16)),
            pltpu.SemaphoreType.DMA((4,)),
            pltpu.SemaphoreType.DMA((4,)),
            pltpu.SemaphoreType.DMA,
        ],
        compiler_params=pltpu.CompilerParams(
            collective_id=0, has_side_effects=True, vmem_limit_bytes=32 << 20
        ),
    )(payload, points, weights, coords, values)


def pair_kernel(
    spot_ref, table, gathered, points, points2, weights, weights2, coords, coords2, values, values2,
    out, left, right, norm, wcat, near_pairs, far_pairs,
):
    scale = LOG2E / 32.0

    def put_source(block, start, width):
        scaled = block * (2.0 * scale)
        high, low = split2(scaled)
        right[0:DIM, pl.ds(start, width)] = high
        right[DIM : 2 * DIM, pl.ds(start, width)] = high
        right[2 * DIM : 3 * DIM, pl.ds(start, width)] = low
        right[3 * DIM : 4 * DIM, pl.ds(start, width)] = jnp.full((DIM, width), -1.0, BF16)
        norm[:, pl.ds(start, width)] = -scale * jnp.sum(block * block, axis=0, keepdims=True)

    def put_weights(block, start, rows):
        high, low = split2(block)
        wcat[pl.ds(start, rows), 0:WCOL] = high
        wcat[pl.ds(start, rows), WCOL : 2 * WCOL] = low

    def sources(n, _):
        at = pl.multiple_of(n * LEAF, LEAF)
        put_source(points[:, pl.ds(at, LEAF)], at, LEAF)
        put_source(points2[:, pl.ds(at, LEAF)], pl.multiple_of(COLPTS + at, LEAF), LEAF)
        put_weights(weights[pl.ds(at, LEAF), :], at, LEAF)
        put_weights(weights2[pl.ds(at, LEAF), :], pl.multiple_of(COLPTS + at, LEAF), LEAF)
        return _

    lax.fori_loop(0, LEAVES, sources, 0)
    put_source(coords[...], 2 * COLPTS, SKEL)
    put_source(coords2[...], 2 * COLPTS + SKEL, SKEL)
    put_weights(values[...], 2 * COLPTS, SKEL)
    put_weights(values2[...], 2 * COLPTS + SKEL, SKEL)

    lane = lax.broadcasted_iota(jnp.int32, (HALF, 128), 1)
    first_half = lane < DIM
    first_quarter = lane % DIM < DIM // 2

    def target(t, _):
        spot, leaf = t // MINE, t % MINE
        both = gathered[spot, pl.ds(pl.multiple_of(leaf * HALF, HALF), HALF), :]
        high = both.astype(BF16).astype(F32)
        low = both - high
        high_r, low_r = pltpu.roll(high, DIM, 1), pltpu.roll(low, DIM, 1)
        square = both * both * scale
        down = square + pltpu.roll(square, 32, 1)
        up = square + pltpu.roll(square, 96, 1)
        up_high = up.astype(BF16).astype(F32)
        down_low = down - down.astype(BF16).astype(F32)
        sums = jnp.where(first_quarter, up_high, down_low)
        at = pl.multiple_of(t * LEAF, LEAF)
        left[pl.ds(at, HALF), 0:128] = jnp.where(first_half, high, low_r).astype(BF16)
        left[pl.ds(at, HALF), 128:256] = jnp.where(first_half, high, pltpu.roll(sums, DIM, 1)).astype(BF16)
        at = pl.multiple_of(at + HALF, HALF)
        left[pl.ds(at, HALF), 0:128] = jnp.where(first_half, high_r, low).astype(BF16)
        left[pl.ds(at, HALF), 128:256] = jnp.where(first_half, high_r, sums).astype(BF16)
        out[pl.ds(pl.multiple_of(t * LEAF, LEAF), LEAF), :] = jnp.zeros((LEAF, WCOL), F32)
        return _

    lax.fori_loop(0, TARGETS, target, 0)

    spot = spot_ref[0]

    def note(t, counts):
        near, far = counts
        for slot in range(4):
            source = table[t, 4 * spot + slot]
            near_pairs[near] = t * 64 + source
            near = near + jnp.where(source >= 0, 1, 0)
        for slot in range(2):
            node = table[t, 64 + 2 * spot + slot]
            far_pairs[far] = t * 64 + node
            far = far + jnp.where(node >= 0, 1, 0)
        return near, far

    near_count, far_count = lax.fori_loop(0, TARGETS, note, (0, 0))

    def interact(t, start, width):
        at = pl.multiple_of(t * LEAF, LEAF)
        columns = pl.ds(start, width)
        power = mm(left[pl.ds(at, LEAF), :], right[:, columns]) + norm[:, columns]
        high, low = split2(jnp.exp2(power))
        total = mm(high, wcat[columns, :])
        rest = mm(low, wcat[columns, 0:WCOL])
        out[pl.ds(at, LEAF), :] += total[:, :WCOL] + total[:, WCOL:] + rest

    def near_pair(n, _):
        code = near_pairs[n]
        interact(code // 64, pl.multiple_of((code % 64) * LEAF, LEAF), LEAF)
        return _

    def far_pair(n, _):
        code = far_pairs[n]
        interact(code // 64, pl.multiple_of(2 * COLPTS + (code % 64) * SKEL, SKEL), SKEL)
        return _

    lax.fori_loop(0, near_count, near_pair, 0)
    lax.fori_loop(0, far_count, far_pair, 0)


def pairs(spot, table, gathered, *sources):
    smem = pl.BlockSpec(memory_space=pltpu.SMEM)
    vmem = pl.BlockSpec(memory_space=VMEM)
    return pl.pallas_call(
        pair_kernel,
        out_shape=jax.ShapeDtypeStruct((TARGETS * LEAF, WCOL), F32),
        in_specs=[smem, smem] + [vmem] * 9,
        out_specs=vmem,
        scratch_shapes=[
            VMEM((TARGETS * LEAF, 256), BF16),
            VMEM((4 * DIM, SOURCES), BF16),
            VMEM((1, SOURCES), F32),
            VMEM((SOURCES, 2 * WCOL), BF16),
            pltpu.SMEM((TARGETS * 4 + 1,), jnp.int32),
            pltpu.SMEM((TARGETS * 2 + 1,), jnp.int32),
        ],
        compiler_params=pltpu.CompilerParams(vmem_limit_bytes=62 << 20),
    )(spot, table, gathered, *sources)


QUARTER = LEAF // 4


def scatter_kernel(partial, out, slots, turn, send, recv, turn_send, turn_recv, y_send, y_recv):
    y, z, x, core = place()
    near = [(1, 0), (SIDE - 1, 0), (0, 1), (0, SIDE - 1)]
    peers = [device(y, (z + a) % SIDE, (x + b) % SIDE, core) for a, b in near]
    above, below = device((y + 1) % SIDE, z, x, core), device((y + SIDE - 1) % SIDE, z, x, core)
    greet(peers + [above, below])
    started = []

    def own(k, leaf, first, second):
        az, ax = moved(k, z, x, first, second)
        start = ((az * SIDE + ax) * MINE + leaf) * LEAF + k * QUARTER
        return pl.ds(pl.multiple_of(start, QUARTER), QUARTER)

    def begin(c):
        c.start()
        started.append(c)

    def step_first(k, leaf, step, j, source):
        tz, tx = moved(k, z, x, 1, 0)
        n = (leaf * 3 + step) * SIDE + j
        begin(pltpu.make_async_remote_copy(
            src_ref=source, dst_ref=slots.at[k, n], send_sem=send.at[k, n], recv_sem=recv.at[k, n],
            device_id=device(y, tz, tx, core), device_id_type=MESH,
        ))

    def arrived_first(k, leaf, step, j):
        n = (leaf * 3 + step) * SIDE + j
        pltpu.make_async_copy(slots.at[k, n], slots.at[k, n], recv.at[k, n]).wait()
        slots[k, n] += partial[own(k, leaf, 2 - step, 3 - j), :]
        return n

    def step_second(k, leaf, step, source):
        tz, tx = moved(k, z, x, 0, 1)
        n = leaf * 3 + step
        begin(pltpu.make_async_remote_copy(
            src_ref=source, dst_ref=turn.at[k, n], send_sem=turn_send.at[k, n], recv_sem=turn_recv.at[k, n],
            device_id=device(y, tz, tx, core), device_id_type=MESH,
        ))

    def rows_of(plane, leaf, k):
        return pl.ds(pl.multiple_of((plane * MINE + leaf) * LEAF + k * QUARTER, QUARTER), QUARTER)

    def to_y(leaf, k, number, plane, up):
        rows = rows_of(plane, leaf, k)
        n = (leaf * 4 + k) * 3 + number
        begin(pltpu.make_async_remote_copy(
            src_ref=out.at[rows], dst_ref=out.at[rows], send_sem=y_send.at[n], recv_sem=y_recv.at[n],
            device_id=above if up else below, device_id_type=MESH,
        ))

    def y_wait(leaf, k, number, plane):
        rows = rows_of(plane, leaf, k)
        n = (leaf * 4 + k) * 3 + number
        pltpu.make_async_copy(out.at[rows], out.at[rows], y_recv.at[n]).wait()

    def second_axis(k, leaf, j):
        n = arrived_first(k, leaf, 2, j)
        if j > 0:
            m = leaf * 3 + j - 1
            pltpu.make_async_copy(turn.at[k, m], turn.at[k, m], turn_recv.at[k, m]).wait()
        if j == 0:
            step_second(k, leaf, 0, slots.at[k, n])
        elif j < 3:
            turn[k, m] += slots[k, n]
            step_second(k, leaf, j, turn.at[k, m])
        else:
            out[rows_of(y, leaf, k), :] = turn[k, m] + slots[k, n]
            to_y(leaf, k, 0, y, True)
            to_y(leaf, k, 1, y, False)

    def second_hop(leaf, k):
        lower, upper = (y + SIDE - 1) % SIDE, (y + 1) % SIDE
        if k % 2 == 0:
            y_wait(leaf, k, 0, lower)
            to_y(leaf, k, 2, lower, True)
        else:
            y_wait(leaf, k, 1, upper)
            to_y(leaf, k, 2, upper, False)

    def last_arrivals(leaf, k):
        lower, upper, across = (y + SIDE - 1) % SIDE, (y + 1) % SIDE, (y + 2) % SIDE
        if k % 2 == 0:
            y_wait(leaf, k, 1, upper)
        else:
            y_wait(leaf, k, 0, lower)
        y_wait(leaf, k, 2, across)

    for leaf in range(MINE + 1):
        if leaf < MINE:
            for j in range(SIDE):
                for k in range(4):
                    step_first(k, leaf, 0, j, partial.at[own(k, leaf, 3, 3 - j)])
        for j in range(SIDE):
            for k in range(4):
                if leaf < MINE:
                    n = arrived_first(k, leaf, 0, j)
                    step_first(k, leaf, 1, j, slots.at[k, n])
                if leaf > 0:
                    second_axis(k, leaf - 1, j)
        if leaf < MINE:
            for j in range(SIDE):
                for k in range(4):
                    n = arrived_first(k, leaf, 1, j)
                    step_first(k, leaf, 2, j, slots.at[k, n])
        if leaf > 0:
            for k in range(4):
                second_hop(leaf - 1, k)
    for leaf in range(MINE):
        for k in range(4):
            last_arrivals(leaf, k)
    for c in started:
        c.wait_send()


def scatter(partial):
    vmem = pl.BlockSpec(memory_space=VMEM)
    return pl.pallas_call(
        scatter_kernel,
        out_shape=jax.ShapeDtypeStruct((COLPTS, WCOL), F32),
        in_specs=[vmem],
        out_specs=vmem,
        scratch_shapes=[
            VMEM((4, MINE * 3 * SIDE, QUARTER, WCOL), F32),
            VMEM((4, MINE * 3, QUARTER, WCOL), F32),
            pltpu.SemaphoreType.DMA((4, MINE * 3 * SIDE)),
            pltpu.SemaphoreType.DMA((4, MINE * 3 * SIDE)),
            pltpu.SemaphoreType.DMA((4, MINE * 3)),
            pltpu.SemaphoreType.DMA((4, MINE * 3)),
            pltpu.SemaphoreType.DMA((MINE * 4 * 3,)),
            pltpu.SemaphoreType.DMA((MINE * 4 * 3,)),
        ],
        compiler_params=pltpu.CompilerParams(
            collective_id=1, has_side_effects=True, vmem_limit_bytes=60 << 20
        ),
    )(partial)


def lists(y, core, fetch_table, near_list, far_list):
    near = lax.dynamic_slice_in_dim(near_list, y * MINE, MINE, 0)
    far = lax.dynamic_slice_in_dim(far_list, y * MINE, MINE, 0)
    slots = jnp.arange(64, dtype=jnp.int32)
    nodes = jnp.arange(32, dtype=jnp.int32)
    near_used = jnp.any(near[:, :, None] == slots, axis=1)
    far_used = jnp.any(far[:, :, None] == nodes, axis=1)
    rows = (y * MINE + jnp.arange(MINE, dtype=jnp.int32)) // 4
    requests = fetch_table[:, 0].reshape(3, 64)
    local = jnp.sum(jnp.where(rows[:, None, None] == jnp.arange(3)[None, :, None], requests[None], 0), axis=1)
    side = (slots // 2 + core) % 2
    near_value = jnp.where(near_used, side * LEAVES + local, -1)
    far_value = jnp.where(far_used, (nodes + core) % 2, -1)
    table = jnp.concatenate([near_value, far_value, jnp.full((MINE, 32), -1, jnp.int32)], axis=1)
    return jnp.pad(table, ((0, 8 - MINE), (0, 0))).astype(F32)


def on_device(points, weights, proj, fetch_table, near_list, far_list, skel_idx):
    y, z, x, core = place()
    table = lists(y, core, fetch_table, near_list, far_list)
    payload, coords, values = prepare(
        y.reshape(1).astype(jnp.int32), points, weights, proj, skel_idx, table
    )
    gathered, points2, weights2, coords2, values2 = gather(payload, points, weights, coords, values)
    found = gathered[:, MINE * HALF : MINE * HALF + MINE, :].astype(jnp.int32).reshape(TARGETS, 128)
    spot = (z * SIDE + x).reshape(1).astype(jnp.int32)
    partial = pairs(
        spot, found, gathered, points, points2, weights, weights2, coords, coords2, values, values2
    )
    return scatter(partial)


def solution(mesh):
    placed = (
        P(None, "dev"),
        P("dev", None),
        P(None, "dev"),
        P(None, "dev", None, None),
        P("dev", None),
        P("dev", None),
        P("dev", None),
    )
    return jax.shard_map(
        on_device, mesh=mesh, in_specs=placed, out_specs=P("dev", None), check_vma=False
    )
```

time: 823 us -> 242 us (0.29)
  waiting for transfers between devices: 507 us -> 0 us
  Pallas kernels: 0 us -> 220 us
  matrix products: 154 us -> 0 us
  local copies, waits for them, and re-layouts: 96.2 us -> 20.2 us
  other arithmetic: 22.5 us -> 0.49 us
  starting transfers between devices: 18.5 us -> 0 us
  between operations: 13.5 us -> 0.09 us
    psum x2 -> x0, waiting for transfers between devices: 415 us -> none  [the longest x1 311 us: on_device(): lax.psum((table_coords, table_weights), ('grp', 'dev'))]
    pallas_call x0 -> x4, Pallas kernels: none -> 220 us  [the longest x1 97.2 us: scatter(): pl.pallas_call(scatter_kernel, out_shape=jax.ShapeDtypeStruct((COLPTS, WC...]
    dot_general x9 -> x0, matrix products: 154 us -> none  [the longest x4 86.1 us: kernel_sum(): return jnp.einsum('tjs,jsw->tw', kernel, values, precision=high)]
    all_to_all x3 -> x0, waiting for transfers between devices: 91.6 us -> none  [the longest x1 86.9 us: on_device(): lax.all_to_all(coords, 'dev', split_axis=0, concat_axis=0, tiled=True)]
    gather x12 -> x0, local copies, waits for them, and re-layouts: 66 us -> none  [the longest x4 34 us: near_leaf(): jnp.take(flat_values, leaf_slots, axis=0)]
    select_n x8 -> x4, other arithmetic: 20.1 us -> 0.04 us  [the longest x2 0.02 us: lists(): far_value = jnp.where(far_used, (nodes + core) % 2, -1)]
    all_to_all x3 -> x0, starting transfers between devices: 18.4 us -> none  [the longest x1 8.25 us: on_device(): lax.all_to_all(requests, 'dev', split_axis=0, concat_axis=0, tiled=True)]
    unnamed x12 -> x28, local copies, waits for them, and re-layouts: 7.05 us -> 18.6 us
  transfers between devices with their start and end apart: 5 -> 0, of which waited for: 4 -> 0; matrix products, arithmetic and copies ran while one was open for 5% -> 0% of each run, Pallas kernels for 0% -> 0%
where the time goes in v1:
time: 242 us; the launch traced here: 240 us
  Pallas kernels  220 us (91%)
  local copies, waits for them, and re-layouts  20.2 us (8%)
    pallas_call x1, Pallas kernels, scatter(): pl.pallas_call(scatter_kernel, out_shape=jax.ShapeDtypeStruct((COLPTS, WC...  97.2 us
    pallas_call x1, Pallas kernels, pairs(): pl.pallas_call(pair_kernel, out_shape=jax.ShapeDtypeStruct((TARGETS * LEA...  70 us
    pallas_call x1, Pallas kernels, gather(): pl.pallas_call(gather_kernel, out_shape=(jax.ShapeDtypeStruct((SPOTS, PAY...  46.3 us
    unnamed x28, local copies, waits for them, and re-layouts  18.6 us
    pallas_call x1, Pallas kernels, prepare(): pl.pallas_call(prepare_kernel, out_shape=(jax.ShapeDtypeStruct((PAYLOAD,...  6.14 us

profile of v1, /device:TPU:0, one launch (start us, length us, event | category | flops | bytes accessed | tf_op | source)
XLA Modules:
  0.0 240.4 jit_solution(5818800147666593436)
XLA Ops:
  0.0 0.0 copy-start
  0.0 0.1 iota_compare_fusion.2
  0.1 0.6 copy-done
  0.7 0.1 fusion
  0.8 0.8 constant_dynamic-slice_fusion
  1.6 0.1 copy.12
  1.6 0.1 fusion.1
  1.7 0.8 copy.11
  2.5 0.1 broadcast_in_dim.43
  2.6 0.1 select_reduce_fusion
  2.7 0.1 pad_add_fusion
  2.8 1.9 copy-done.1
  4.7 1.4 copy-done.3
  6.1 2.8 %copy-done.5 = f32[256,6144]{1,0:T(8,128)S(1)} copy-done((f32[256,6144]{1,0:T(8,128)S(1)}, f32[256,6144]{1,0:T(8,128)}, u32[]{:S(2)}) %copy-start.5) | copy-done | bytes 6291480
  8.9 0.7 copy-done.12
  9.6 6.1 %shard_map.73 = (f32[776,128]{1,0:T(8,128)S(1)}, f32[64,256]{1,0:T(8,128)S(1)}, f32[256,128]{1,0:T(8,128)S(1)}) custom-call(s32[1]{0:T(128)} %bitcast.1.y_ref, f32[64,6144]{1,0:T(8,128)S(1)} %copy-done.3, f32[6144,128]{1,0:T(8,128)S(1)} %copy-done.1, f32[256,6144]{1,0:T(8,128)S(1)} %copy-done.5, s32[1,256]{1,0:T(1,128)S(1)} %copy-done.12, ...), custom_call_target="tpu_custom_call" | custom-call | tf_op jit(solution)/shard_map/pallas_call | solution.py:68
  15.7 0.0 copy-start.8
  15.8 0.0 copy-start.9
  15.8 0.0 copy-done.2
  15.8 46.3 %shard_map.74 = (f32[16,776,128]{2,1,0:T(8,128)S(1)}, f32[64,6144]{1,0:T(8,128)S(1)}, f32[6144,128]{1,0:T(8,128)S(1)}, f32[64,256]{1,0:T(8,128)S(1)}, f32[256,128]{1,0:T(8,128)S(1)}) custom-call(f32[776,128]{1,0:T(8,128)S(1)} %get-tuple-element.13.payload, f32[64,6144]{1,0:T(8,128)S(1)} %copy-done.3, f32[6144,128]{1,0:T(8,128)S(1)} %copy-done.2, ...), custom_call_target="tpu_custom_call" | custom-call | tf_op jit(solution)/shard_map/pallas_call | solution.py:195
  62.0 0.0 copy-start.6
  62.1 1.7 copy-done.6
  63.7 1.2 copy-done.7
  64.9 0.7 copy-done.10
  65.5 0.6 copy-done.11
  66.2 2.6 %copy-done.4 = f32[16,776,128]{2,1,0:T(8,128)} copy-done((f32[16,776,128]{2,1,0:T(8,128)}, f32[16,776,128]{2,1,0:T(8,128)S(1)}, u32[]{:S(2)}) %copy-start.4) | copy-done | bytes 6357016
  68.8 0.6 reshape.83.table
  69.4 0.0 copy-done.8
  69.4 0.0 copy-done.9
  69.4 70.0 %shard_map.75.partial = f32[24576,128]{1,0:T(8,128)} custom-call(s32[1]{0:T(128)} %bitcast.spot_ref, s32[48,128]{1,0:T(8,128)} %reshape.83.table, f32[16,776,128]{2,1,0:T(8,128)} %copy-done.4, f32[64,6144]{1,0:T(8,128)} %points.5, f32[64,6144]{1,0:T(8,128)} %copy-done.7, f32[6144,128]{1,0:T(8,128)} %weights.5, f32[6144,128]{1,0:T(8,128)} %copy-done.6, ...), custom_call_target="tpu_custom_call" | custom-call | tf_op jit(solution)/shard_map/pallas_call | solution.py:322
  139.5 97.2 %shard_map.76 = f32[6144,128]{1,0:T(8,128)} custom-call(f32[24576,128]{1,0:T(8,128)} %shard_map.75.partial), custom_call_target="tpu_custom_call" | custom-call | tf_op jit(solution)/shard_map/pallas_call | solution.py:458
  236.6 3.8 %copy.14 = f32[6144,128]{1,0:T(8,128)} copy(f32[6144,128]{1,0:T(8,128)} %shard_map.76) | data formatting | bytes 6291456
  (18 shorter events, 0.1 us)
Async XLA Ops:
  0.0 0.7 copy-start
  2.8 1.9 copy-start.1
  4.7 1.4 copy-start.3
  6.1 2.8 %copy-start.5 = (f32[256,6144]{1,0:T(8,128)S(1)}, f32[256,6144]{1,0:T(8,128)}, u32[]{:S(2)}) copy-start(f32[256,6144]{1,0:T(8,128)} %proj.1) | copy-start | bytes 18874372
  8.9 0.7 copy-start.12
  9.6 6.2 %copy-start.2 = (f32[6144,128]{1,0:T(8,128)S(1)}, f32[6144,128]{1,0:T(8,128)}, u32[]{:S(2)}) copy-start(f32[6144,128]{1,0:T(8,128)} %weights.5) | copy-start | bytes 9437188
  15.7 53.7 %copy-start.8 = (f32[256,128]{1,0:T(8,128)}, f32[256,128]{1,0:T(8,128)S(1)}, u32[]{:S(2)}) copy-start(f32[256,128]{1,0:T(8,128)S(1)} %get-tuple-element.15.values) | copy-start | bytes 393220
  15.8 53.7 %copy-start.9 = (f32[64,256]{1,0:T(8,128)}, f32[64,256]{1,0:T(8,128)S(1)}, u32[]{:S(2)}) copy-start(f32[64,256]{1,0:T(8,128)S(1)} %get-tuple-element.14.coords) | copy-start | bytes 196612
  62.0 1.7 copy-start.6
  63.7 1.2 copy-start.7
  64.9 0.7 copy-start.10
  65.5 0.6 copy-start.11
  66.2 2.6 %copy-start.4 = (f32[16,776,128]{2,1,0:T(8,128)}, f32[16,776,128]{2,1,0:T(8,128)S(1)}, u32[]{:S(2)}) copy-start(f32[16,776,128]{2,1,0:T(8,128)S(1)} %get-tuple-element.16.gathered) | copy-start | bytes 19070980

commit v2 on v1

v2 whole, which is shorter than its diff:
```python
import functools
import math

import jax
import jax.numpy as jnp
from jax import lax
from jax.experimental import pallas as pl
from jax.experimental.pallas import tpu as pltpu
from jax.sharding import PartitionSpec as P

F32, BF16 = jnp.float32, jnp.bfloat16
MESH = pl.DeviceIdType.MESH
VMEM = pltpu.VMEM
LOG2E = math.log2(math.e)
SIDE = 4
SPOTS = SIDE * SIDE
LEAF, DIM, WCOL, SKEL = 512, 64, 128, 256
LEAVES = 12
MINE = 3
COLPTS = LEAVES * LEAF
HALF = LEAF // 2
PAYLOAD = MINE * HALF + 8
TARGETS = SPOTS * MINE
SOURCES = 2 * COLPTS + 2 * SKEL
CHUNK = 1024
SCALE = LOG2E / 32.0
K1_VMEM, K2_VMEM, K3_VMEM = 30 << 20, 8 << 20, 30 << 20
CUTS = (0, 192, 384, 576, PAYLOAD)


def mm(a, b):
    return jnp.dot(a, b, preferred_element_type=F32)


def split2(v):
    high = v.astype(BF16)
    return high, (v - high.astype(F32)).astype(BF16)


def place():
    y, dev = lax.axis_index("grp"), lax.axis_index("dev")
    return y, dev // 8, (dev // 2) % SIDE, dev % 2


def device(y, z, x, core):
    return (y, (z * SIDE + x) * 2 + core)


def stream_axes(k):
    return k < 2, 1 if k % 2 == 0 else SIDE - 1


def moved(k, z, x, first, second):
    x_first, sign = stream_axes(k)
    along_x, along_z = (first, second) if x_first else (second, first)
    return (z + sign * along_z) % SIDE, (x + sign * along_x) % SIDE


def greet(peers):
    barrier = pltpu.get_barrier_semaphore()
    for peer in peers:
        pl.semaphore_signal(barrier, inc=1, device_id=peer, device_id_type=MESH)
    pl.semaphore_wait(barrier, len(peers))


def put_source(block, right, norm, start):
    width = block.shape[1]
    high, low = split2(block * (2.0 * SCALE))
    right[0:DIM, pl.ds(start, width)] = high
    right[DIM : 2 * DIM, pl.ds(start, width)] = high
    right[2 * DIM : 3 * DIM, pl.ds(start, width)] = low
    right[3 * DIM : 4 * DIM, pl.ds(start, width)] = jnp.full((DIM, width), -1.0, BF16)
    norm[:, pl.ds(start, width)] = -SCALE * jnp.sum(block * block, axis=0, keepdims=True)


def put_weights(block, wcat, start):
    high, low = split2(block)
    wcat[pl.ds(start, block.shape[0]), 0:WCOL] = high
    wcat[pl.ds(start, block.shape[0]), WCOL : 2 * WCOL] = low


def put_target(both, left, at):
    lane = lax.broadcasted_iota(jnp.int32, both.shape, 1)
    first_half = lane < DIM
    first_quarter = lane % DIM < DIM // 2
    high = both.astype(BF16).astype(F32)
    low = both - high
    high_r, low_r = pltpu.roll(high, DIM, 1), pltpu.roll(low, DIM, 1)
    square = both * both * SCALE
    down = square + pltpu.roll(square, 32, 1)
    up = square + pltpu.roll(square, 96, 1)
    up_high = up.astype(BF16).astype(F32)
    down_low = down - down.astype(BF16).astype(F32)
    sums = jnp.where(first_quarter, up_high, down_low)
    left[pl.ds(at, HALF), 0:128] = jnp.where(first_half, high, low_r).astype(BF16)
    left[pl.ds(at, HALF), 128:256] = jnp.where(first_half, high, pltpu.roll(sums, DIM, 1)).astype(BF16)
    left[pl.ds(at + HALF, HALF), 0:128] = jnp.where(first_half, high_r, low).astype(BF16)
    left[pl.ds(at + HALF, HALF), 128:256] = jnp.where(first_half, high_r, sums).astype(BF16)


def gather_kernel(
    points_hbm, weights_hbm, proj_hbm, index, table,
    left, right, norm, wcat, found,
    payload, gathered, own, points, points2, weights, weights2, proj, coords, coords2, values, values2,
    send, recv, pair_send, pair_recv, load_sem,
):
    y, z, x, core = place()
    loads = [
        pltpu.make_async_copy(
            points_hbm.at[:, pl.ds(pl.multiple_of(y * (MINE * LEAF), LEAF), MINE * LEAF)], own, load_sem.at[0]
        ),
        pltpu.make_async_copy(points_hbm, points, load_sem.at[1]),
        pltpu.make_async_copy(weights_hbm, weights, load_sem.at[2]),
        pltpu.make_async_copy(proj_hbm, proj, load_sem.at[3]),
    ]
    for c in loads:
        c.start()
    near = [(1, 0), (SIDE - 1, 0), (0, 1), (0, SIDE - 1)]
    peers = [device(y, (z + a) % SIDE, (x + b) % SIDE, core) for a, b in near]
    sibling = device(y, z, x, 1 - core)
    greet(peers + [sibling])

    loads[0].wait()
    for leaf in range(MINE):
        block = own[:, leaf * LEAF : (leaf + 1) * LEAF]
        packed = jnp.concatenate([block[:, :HALF], block[:, HALF:]], axis=0)
        payload[leaf * HALF : (leaf + 1) * HALF, :] = packed.T
    payload[MINE * HALF :, :] = table[...]

    started, swaps = [], []

    def spot_of(k, i, j):
        az, ax = moved(k, z, x, -i, -j)
        return az * SIDE + ax

    def copy(k, i, j, first):
        rows = pl.ds(CUTS[k], CUTS[k + 1] - CUTS[k])
        tz, tx = moved(k, z, x, 1 if first else 0, 0 if first else 1)
        arrival = (i + 1) * SIDE + j if first else i * SIDE + j + 1
        number = i if first else SIDE - 1 + i * (SIDE - 1) + j
        target = gathered.at[spot_of(k, i, j), rows]
        c = pltpu.make_async_remote_copy(
            src_ref=payload.at[rows] if i == 0 and j == 0 else target,
            dst_ref=target,
            send_sem=send.at[k, number],
            recv_sem=recv.at[k, arrival],
            device_id=device(y, tz, tx, core),
            device_id_type=MESH,
        )
        c.start()
        started.append(c)

    def forward(level):
        for i in range(SIDE):
            j = level - i
            if not 0 <= j < SIDE:
                continue
            for k in range(4):
                if level > 0:
                    rows = pl.ds(CUTS[k], CUTS[k + 1] - CUTS[k])
                    here = gathered.at[spot_of(k, i, j), rows]
                    pltpu.make_async_copy(here, here, recv.at[k, i * SIDE + j]).wait()
                if j == 0 and i < SIDE - 1:
                    copy(k, i, j, True)
                if j < SIDE - 1:
                    copy(k, i, j, False)

    def swap(n, a, b):
        c = pltpu.make_async_remote_copy(
            src_ref=a, dst_ref=b, send_sem=pair_send.at[n], recv_sem=pair_recv.at[n],
            device_id=sibling, device_id_type=MESH,
        )
        c.start()
        swaps.append(c)

    def targets_at(dz, dx):
        spot = (z + dz) % SIDE * SIDE + (x + dx) % SIDE

        def leaf_rows(leaf, _):
            rows = pl.ds(pl.multiple_of(leaf * HALF, HALF), HALF)
            both = payload[rows, :] if dz == dx == 0 else gathered[spot, rows, :]
            put_target(both, left, pl.multiple_of((spot * MINE + leaf) * LEAF, LEAF))
            return _

        lax.fori_loop(0, MINE, leaf_rows, 0)
        lists_here = payload[MINE * HALF :, :] if dz == dx == 0 else gathered[spot, MINE * HALF :, :]
        found[spot] = lists_here.astype(jnp.int32)

    def column(points_ref, weights_ref, base):
        def one(n, _):
            at = pl.multiple_of(n * LEAF, LEAF)
            put_source(points_ref[:, pl.ds(at, LEAF)], right, norm, pl.multiple_of(base + at, LEAF))
            put_weights(weights_ref[pl.ds(at, LEAF), :], wcat, pl.multiple_of(base + at, LEAF))
            return _

        lax.fori_loop(0, LEAVES, one, 0)

    def spots_of(level):
        steps = (0, 1, 2, 3)

        def done(dz, dx):
            far = lambda d: max(d, (SIDE - d) % SIDE)
            return far(dz) + far(dx)

        return [(dz, dx) for dz in steps for dx in steps if done(dz, dx) == level]

    forward(0)
    loads[1].wait()
    loads[2].wait()
    swap(0, points, points2)
    swap(1, weights, weights2)
    targets_at(0, 0)
    column(points, weights, 0)
    forward(1)
    loads[3].wait()
    values[...] = jnp.zeros_like(values)
    coords[...] = jnp.zeros_like(coords)

    def skeleton(n, _):
        at = pl.multiple_of(n * CHUNK, CHUNK)
        wh, wl = wcat[pl.ds(at, CHUNK), 0:WCOL], wcat[pl.ds(at, CHUNK), WCOL : 2 * WCOL]
        ph, plow = split2(proj[:, pl.ds(at, CHUNK)])
        values[...] += mm(ph, wh) + mm(ph, wl) + mm(plow, wh)
        rows = lax.broadcasted_iota(jnp.int32, (CHUNK, SKEL), 0) + at
        pick = jnp.where(rows == index[...], 1.0, 0.0).astype(BF16)
        block = points[:, pl.ds(at, CHUNK)]
        first = block.astype(BF16)
        second, third = split2(block - first.astype(F32))
        coords[...] += mm(first, pick) + mm(second, pick) + mm(third, pick)
        return _

    lax.fori_loop(0, COLPTS // CHUNK, skeleton, 0)
    swap(2, coords, coords2)
    swap(3, values, values2)
    forward(2)
    put_source(coords[...], right, norm, 2 * COLPTS)
    put_weights(values[...], wcat, 2 * COLPTS)
    swaps[0].wait_recv()
    swaps[1].wait_recv()
    column(points2, weights2, COLPTS)
    forward(3)
    swaps[2].wait_recv()
    swaps[3].wait_recv()
    put_source(coords2[...], right, norm, 2 * COLPTS + SKEL)
    put_weights(values2[...], wcat, 2 * COLPTS + SKEL)
    for level in (2, 3):
        for dz, dx in spots_of(level):
            targets_at(dz, dx)
    for level in (4, 5, 6):
        forward(level)
        for dz, dx in spots_of(level):
            targets_at(dz, dx)
    for c in started + swaps:
        c.wait_send()


def gather(points, weights, proj, index, table):
    anywhere = pl.BlockSpec(memory_space=pl.ANY)
    vmem = pl.BlockSpec(memory_space=VMEM)
    return pl.pallas_call(
        gather_kernel,
        out_shape=(
            pltpu.VMEM((TARGETS * LEAF, 256), BF16),
            pltpu.VMEM((4 * DIM, SOURCES), BF16),
            pltpu.VMEM((1, SOURCES), F32),
            pltpu.VMEM((SOURCES, 2 * WCOL), BF16),
            jax.ShapeDtypeStruct((SPOTS, 8, 128), jnp.int32),
        ),
        in_specs=[anywhere] * 3 + [vmem] * 2,
        out_specs=[vmem] * 5,
        scratch_shapes=[
            VMEM((PAYLOAD, 128), F32),
            VMEM((SPOTS, PAYLOAD, 128), F32),
            VMEM((DIM, MINE * LEAF), F32),
            VMEM((DIM, COLPTS), F32),
            VMEM((DIM, COLPTS), F32),
            VMEM((COLPTS, WCOL), F32),
            VMEM((COLPTS, WCOL), F32),
            VMEM((SKEL, COLPTS), F32),
            VMEM((DIM, SKEL), F32),
            VMEM((DIM, SKEL), F32),
            VMEM((SKEL, WCOL), F32),
            VMEM((SKEL, WCOL), F32),
            pltpu.SemaphoreType.DMA((4, 15)),
            pltpu.SemaphoreType.DMA((4, 16)),
            pltpu.SemaphoreType.DMA((4,)),
            pltpu.SemaphoreType.DMA((4,)),
            pltpu.SemaphoreType.DMA((4,)),
        ],
        compiler_params=pltpu.CompilerParams(
            collective_id=0, has_side_effects=True, vmem_limit_bytes=K1_VMEM
        ),
    )(points, weights, proj, index, table)


def pair_kernel(spot_ref, table, left, right, norm, wcat, out, even, even_low, odd, odd_low, near_pairs, far_pairs):
    def zero(t, _):
        out[pl.ds(pl.multiple_of(t * LEAF, LEAF), LEAF), :] = jnp.zeros((LEAF, WCOL), F32)
        return _

    lax.fori_loop(0, TARGETS + 1, zero, 0)
    spot = spot_ref[0]

    def note(t, counts):
        near, far = counts
        for slot in range(4):
            source = table[t // MINE, t % MINE, 4 * spot + slot]
            near_pairs[near] = t * 64 + source
            near = near + jnp.where(source >= 0, 1, 0)
        for slot in range(2):
            node = table[t // MINE, t % MINE, 64 + 2 * spot + slot]
            far_pairs[far] = t * 64 + node
            far = far + jnp.where(node >= 0, 1, 0)
        return near, far

    near_count, far_count = lax.fori_loop(0, TARGETS, note, (0, 0))
    for extra in range(3):
        near_pairs[near_count + extra] = TARGETS * 64
        far_pairs[far_count + extra] = TARGETS * 64

    def run(pair_list, count, base, width):
        def columns(code):
            return pl.ds(pl.multiple_of(base + (code % 64) * width, width), width)

        def produce(n, high_ref, low_ref):
            code = pair_list[n]
            t, where = code // 64, columns(code)
            at = pl.multiple_of(jnp.where(t < TARGETS, t, 0) * LEAF, LEAF)
            power = mm(left[pl.ds(at, LEAF), :], right[:, where]) + norm[:, where]
            high_ref[:, :width], low_ref[:, :width] = split2(jnp.exp2(power))

        def consume(n, high_ref, low_ref):
            code = pair_list[n]
            t, where = code // 64, columns(code)
            total = mm(high_ref[:, :width], wcat[where, :])
            rest = mm(low_ref[:, :width], wcat[where, 0:WCOL])
            at = pl.multiple_of(t * LEAF, LEAF)
            out[pl.ds(at, LEAF), :] += total[:, :WCOL] + total[:, WCOL:] + rest

        produce(0, even, even_low)

        def two(m, _):
            produce(2 * m + 1, odd, odd_low)
            consume(2 * m, even, even_low)
            produce(2 * m + 2, even, even_low)
            consume(2 * m + 1, odd, odd_low)
            return _

        lax.fori_loop(0, (count + 1) // 2, two, 0)

    run(near_pairs, near_count, 0, LEAF)
    run(far_pairs, far_count, 2 * COLPTS, SKEL)


def pairs(spot, table, left, right, norm, wcat):
    smem = pl.BlockSpec(memory_space=pltpu.SMEM)
    vmem = pl.BlockSpec(memory_space=VMEM)
    return pl.pallas_call(
        pair_kernel,
        out_shape=pltpu.VMEM(((TARGETS + 1) * LEAF, WCOL), F32),
        in_specs=[smem, smem] + [vmem] * 4,
        out_specs=vmem,
        scratch_shapes=[VMEM((LEAF, LEAF), BF16)] * 4
        + [
            pltpu.SMEM((TARGETS * 4 + 3,), jnp.int32),
            pltpu.SMEM((TARGETS * 2 + 3,), jnp.int32),
        ],
        compiler_params=pltpu.CompilerParams(vmem_limit_bytes=K2_VMEM),
    )(spot, table, left, right, norm, wcat)


QUARTER = LEAF // 4


def scatter_kernel(partial, out, slots, turn, send, recv, turn_send, turn_recv, y_send, y_recv):
    y, z, x, core = place()
    near = [(1, 0), (SIDE - 1, 0), (0, 1), (0, SIDE - 1)]
    peers = [device(y, (z + a) % SIDE, (x + b) % SIDE, core) for a, b in near]
    above, below = device((y + 1) % SIDE, z, x, core), device((y + SIDE - 1) % SIDE, z, x, core)
    greet(peers + [above, below])
    started = []

    def own(k, leaf, first, second):
        az, ax = moved(k, z, x, first, second)
        start = ((az * SIDE + ax) * MINE + leaf) * LEAF + k * QUARTER
        return pl.ds(pl.multiple_of(start, QUARTER), QUARTER)

    def begin(c):
        c.start()
        started.append(c)

    def step_first(k, leaf, step, j, source):
        tz, tx = moved(k, z, x, 1, 0)
        n = (leaf * 3 + step) * SIDE + j
        begin(pltpu.make_async_remote_copy(
            src_ref=source, dst_ref=slots.at[k, n], send_sem=send.at[k, n], recv_sem=recv.at[k, n],
            device_id=device(y, tz, tx, core), device_id_type=MESH,
        ))

    def arrived_first(k, leaf, step, j):
        n = (leaf * 3 + step) * SIDE + j
        pltpu.make_async_copy(slots.at[k, n], slots.at[k, n], recv.at[k, n]).wait()
        slots[k, n] += partial[own(k, leaf, 2 - step, 3 - j), :]
        return n

    def step_second(k, leaf, step, source):
        tz, tx = moved(k, z, x, 0, 1)
        n = leaf * 3 + step
        begin(pltpu.make_async_remote_copy(
            src_ref=source, dst_ref=turn.at[k, n], send_sem=turn_send.at[k, n], recv_sem=turn_recv.at[k, n],
            device_id=device(y, tz, tx, core), device_id_type=MESH,
        ))

    def rows_of(plane, leaf, k):
        return pl.ds(pl.multiple_of((plane * MINE + leaf) * LEAF + k * QUARTER, QUARTER), QUARTER)

    def to_y(leaf, k, number, plane, up):
        rows = rows_of(plane, leaf, k)
        n = (leaf * 4 + k) * 3 + number
        begin(pltpu.make_async_remote_copy(
            src_ref=out.at[rows], dst_ref=out.at[rows], send_sem=y_send.at[n], recv_sem=y_recv.at[n],
            device_id=above if up else below, device_id_type=MESH,
        ))

    def y_wait(leaf, k, number, plane):
        rows = rows_of(plane, leaf, k)
        n = (leaf * 4 + k) * 3 + number
        pltpu.make_async_copy(out.at[rows], out.at[rows], y_recv.at[n]).wait()

    def second_axis(k, leaf, j):
        n = arrived_first(k, leaf, 2, j)
        if j > 0:
            m = leaf * 3 + j - 1
            pltpu.make_async_copy(turn.at[k, m], turn.at[k, m], turn_recv.at[k, m]).wait()
        if j == 0:
            step_second(k, leaf, 0, slots.at[k, n])
        elif j < 3:
            turn[k, m] += slots[k, n]
            step_second(k, leaf, j, turn.at[k, m])
        else:
            out[rows_of(y, leaf, k), :] = turn[k, m] + slots[k, n]
            to_y(leaf, k, 0, y, True)
            to_y(leaf, k, 1, y, False)

    def second_hop(leaf, k):
        lower, upper = (y + SIDE - 1) % SIDE, (y + 1) % SIDE
        if k % 2 == 0:
            y_wait(leaf, k, 0, lower)
            to_y(leaf, k, 2, lower, True)
        else:
            y_wait(leaf, k, 1, upper)
            to_y(leaf, k, 2, upper, False)

    def last_arrivals(leaf, k):
        lower, upper, across = (y + SIDE - 1) % SIDE, (y + 1) % SIDE, (y + 2) % SIDE
        if k % 2 == 0:
            y_wait(leaf, k, 1, upper)
        else:
            y_wait(leaf, k, 0, lower)
        y_wait(leaf, k, 2, across)

    for leaf in range(MINE + 1):
        if leaf < MINE:
            for j in range(SIDE):
                for k in range(4):
                    step_first(k, leaf, 0, j, partial.at[own(k, leaf, 3, 3 - j)])
        for j in range(SIDE):
            for k in range(4):
                if leaf < MINE:
                    n = arrived_first(k, leaf, 0, j)
                    step_first(k, leaf, 1, j, slots.at[k, n])
                if leaf > 0:
                    second_axis(k, leaf - 1, j)
        if leaf < MINE:
            for j in range(SIDE):
                for k in range(4):
                    n = arrived_first(k, leaf, 1, j)
                    step_first(k, leaf, 2, j, slots.at[k, n])
        if leaf > 0:
            for k in range(4):
                second_hop(leaf - 1, k)
    for leaf in range(MINE):
        for k in range(4):
            last_arrivals(leaf, k)
    for c in started:
        c.wait_send()


def scatter(partial):
    vmem = pl.BlockSpec(memory_space=VMEM)
    return pl.pallas_call(
        scatter_kernel,
        out_shape=jax.ShapeDtypeStruct((COLPTS, WCOL), F32),
        in_specs=[vmem],
        out_specs=vmem,
        scratch_shapes=[
            VMEM((4, MINE * 3 * SIDE, QUARTER, WCOL), F32),
            VMEM((4, MINE * 3, QUARTER, WCOL), F32),
            pltpu.SemaphoreType.DMA((4, MINE * 3 * SIDE)),
            pltpu.SemaphoreType.DMA((4, MINE * 3 * SIDE)),
            pltpu.SemaphoreType.DMA((4, MINE * 3)),
            pltpu.SemaphoreType.DMA((4, MINE * 3)),
            pltpu.SemaphoreType.DMA((MINE * 4 * 3,)),
            pltpu.SemaphoreType.DMA((MINE * 4 * 3,)),
        ],
        compiler_params=pltpu.CompilerParams(
            collective_id=1, has_side_effects=True, vmem_limit_bytes=K3_VMEM
        ),
    )(partial)


def lists(y, core, fetch_table, near_list, far_list):
    near = lax.dynamic_slice_in_dim(near_list, y * MINE, MINE, 0)
    far = lax.dynamic_slice_in_dim(far_list, y * MINE, MINE, 0)
    slots = jnp.arange(64, dtype=jnp.int32)
    nodes = jnp.arange(32, dtype=jnp.int32)
    near_used = jnp.any(near[:, :, None] == slots, axis=1)
    far_used = jnp.any(far[:, :, None] == nodes, axis=1)
    rows = (y * MINE + jnp.arange(MINE, dtype=jnp.int32)) // 4
    requests = fetch_table[:, 0].reshape(3, 64)
    local = jnp.sum(jnp.where(rows[:, None, None] == jnp.arange(3)[None, :, None], requests[None], 0), axis=1)
    side = (slots // 2 + core) % 2
    near_value = jnp.where(near_used, side * LEAVES + local, -1)
    far_value = jnp.where(far_used, (nodes + core) % 2, -1)
    table = jnp.concatenate([near_value, far_value, jnp.full((MINE, 32), -1, jnp.int32)], axis=1)
    return jnp.pad(table, ((0, 8 - MINE), (0, 0))).astype(F32)


def on_device(points, weights, proj, fetch_table, near_list, far_list, skel_idx):
    y, z, x, core = place()
    table = lists(y, core, fetch_table, near_list, far_list)
    left, right, norm, wcat, found = gather(points, weights, proj, skel_idx, table)
    spot = (z * SIDE + x).reshape(1).astype(jnp.int32)
    partial = pairs(spot, found, left, right, norm, wcat)
    return scatter(partial)


def solution(mesh):
    placed = (
        P(None, "dev"),
        P("dev", None),
        P(None, "dev"),
        P(None, "dev", None, None),
        P("dev", None),
        P("dev", None),
        P("dev", None),
    )
    return jax.shard_map(
        on_device, mesh=mesh, in_specs=placed, out_specs=P("dev", None), check_vma=False
    )
```

time: 242 us -> 209 us (0.86)
  Pallas kernels: 220 us -> 183 us
  local copies, waits for them, and re-layouts: 20.2 us -> 25.1 us
    pallas_call x3 -> x2, Pallas kernels: 122 us -> 92.6 us  [the longest x1 51 us: gather(): pl.pallas_call(gather_kernel, out_shape=(pltpu.VMEM((TARGETS * LEAF, 256)...]
    pallas_call x1, Pallas kernels: 97.2 us -> 90.2 us  [scatter(): pl.pallas_call(scatter_kernel, out_shape=jax.ShapeDtypeStruct((COLPTS, WC...]
    unnamed x28 -> x18, local copies, waits for them, and re-layouts: 18.6 us -> 24.1 us
where the time goes in v2:
time: 209 us
  Pallas kernels  183 us (88%)
  local copies, waits for them, and re-layouts  25.1 us (12%)
    pallas_call x1, Pallas kernels, scatter(): pl.pallas_call(scatter_kernel, out_shape=jax.ShapeDtypeStruct((COLPTS, WC...  90.2 us
    pallas_call x1, Pallas kernels, gather(): pl.pallas_call(gather_kernel, out_shape=(pltpu.VMEM((TARGETS * LEAF, 256)...  51 us
    pallas_call x1, Pallas kernels, pairs(): pl.pallas_call(pair_kernel, out_shape=pltpu.VMEM(((TARGETS + 1) * LEAF, W...  41.7 us
    unnamed x18, local copies, waits for them, and re-layouts  24.1 us

profile of v2, /device:TPU:0, one launch (start us, length us, event | category | flops | bytes accessed | tf_op | source)
XLA Modules:
  0.0 209.1 jit_solution(14681385978168586904)
XLA Ops:
  0.0 0.0 copy-start
  0.0 0.1 iota_compare_fusion.2
  0.1 0.6 copy-done
  0.7 0.1 fusion
  0.8 0.8 constant_dynamic-slice_fusion
  1.6 0.1 copy.12
  1.6 0.1 fusion.1
  1.7 0.8 copy.11
  2.5 0.1 broadcast_in_dim.43
  2.6 0.1 select_reduce_fusion
  2.7 0.1 pad_add_fusion
  2.8 0.6 pad_convert_fusion.table
  3.4 51.0 %shard_map.73 = (bf16[24576,256]{1,0:T(8,128)(2,1)S(1)}, bf16[256,12800]{1,0:T(8,128)(2,1)S(1)}, f32[1,12800]{1,0:T(1,128)S(1)}, bf16[12800,256]{1,0:T(8,128)(2,1)S(1)}, s32[16,8,128]{2,1,0:T(8,128)}) custom-call(f32[64,6144]{1,0:T(8,128)} %points_hbm.1, f32[6144,128]{1,0:T(8,128)} %weights_hbm.1, f32[256,6144]{1,0:T(8,128)} %proj_hbm.1, s32[1,256]{1,0:T(1,128)} %index.1, ...), custom_call_target="tpu_custom_call" | custom-call | tf_op jit(solution)/shard_map/pallas_call | solution.py:260
  54.4 0.0 copy-start.1
  54.4 4.6 %copy-done.1 = bf16[24576,256]{1,0:T(8,128)(2,1)} copy-done((bf16[24576,256]{1,0:T(8,128)(2,1)}, bf16[24576,256]{1,0:T(8,128)(2,1)S(1)}, u32[]{:S(2)}) %copy-start.1) | copy-done | bytes 12582936
  59.0 0.0 copy-start.3
  59.0 2.7 %copy-done.3 = bf16[256,12800]{1,0:T(8,128)(2,1)} copy-done((bf16[256,12800]{1,0:T(8,128)(2,1)}, bf16[256,12800]{1,0:T(8,128)(2,1)S(1)}, u32[]{:S(2)}) %copy-start.3) | copy-done | bytes 6553624
  61.7 0.0 copy-start.5
  61.7 2.7 %copy-done.5 = bf16[12800,256]{1,0:T(8,128)(2,1)} copy-done((bf16[12800,256]{1,0:T(8,128)(2,1)}, bf16[12800,256]{1,0:T(8,128)(2,1)S(1)}, u32[]{:S(2)}) %copy-start.5) | copy-done | bytes 6553624
  64.4 0.0 copy-start.2
  64.4 4.6 %copy-done.2 = bf16[24576,256]{1,0:T(8,128)(2,1)S(1)} copy-done((bf16[24576,256]{1,0:T(8,128)(2,1)S(1)}, bf16[24576,256]{1,0:T(8,128)(2,1)}, u32[]{:S(2)}) %copy-start.2) | copy-done | bytes 12582936
  69.0 0.0 copy-start.4
  69.0 2.9 %copy-done.4 = bf16[256,12800]{1,0:T(8,128)(2,1)S(1)} copy-done((bf16[256,12800]{1,0:T(8,128)(2,1)S(1)}, bf16[256,12800]{1,0:T(8,128)(2,1)}, u32[]{:S(2)}) %copy-start.4) | copy-done | bytes 6553624
  71.8 0.0 copy-start.6
  71.8 2.9 %copy-done.6 = bf16[12800,256]{1,0:T(8,128)(2,1)S(1)} copy-done((bf16[12800,256]{1,0:T(8,128)(2,1)S(1)}, bf16[12800,256]{1,0:T(8,128)(2,1)}, u32[]{:S(2)}) %copy-start.6) | copy-done | bytes 6553624
  74.7 0.0 copy-start.7
  74.7 0.8 copy-done.7
  75.5 41.7 %shard_map.74.partial = f32[25088,128]{1,0:T(8,128)S(1)} custom-call(s32[1]{0:T(128)} %bitcast.spot_ref, s32[16,8,128]{2,1,0:T(8,128)S(1)} %copy-done.7, bf16[24576,256]{1,0:T(8,128)(2,1)S(1)} %copy-done.2, bf16[256,12800]{1,0:T(8,128)(2,1)S(1)} %copy-done.4, f32[1,12800]{1,0:T(1,128)S(1)} %get-tuple-element.13.norm, bf16[12800,256]{1,0:T(8,128)(2,1)S(1)} %copy-done.6), custom_call_target="tpu_custom_call" | custom-call | tf_op jit(solution)/shard_map/pallas_call | solution.py:358
  117.2 90.2 %shard_map.75 = f32[6144,128]{1,0:T(8,128)S(1)} custom-call(f32[25088,128]{1,0:T(8,128)S(1)} %shard_map.74.partial), custom_call_target="tpu_custom_call" | custom-call | tf_op jit(solution)/shard_map/pallas_call | solution.py:491
  207.4 1.7 copy.14
  (7 shorter events, 0.1 us)
Async XLA Ops:
  0.0 0.7 copy-start
  54.4 4.6 %copy-start.1 = (bf16[24576,256]{1,0:T(8,128)(2,1)}, bf16[24576,256]{1,0:T(8,128)(2,1)S(1)}, u32[]{:S(2)}) copy-start(bf16[24576,256]{1,0:T(8,128)(2,1)S(1)} %get-tuple-element.11.left) | copy-start | bytes 37748740
  59.0 2.7 %copy-start.3 = (bf16[256,12800]{1,0:T(8,128)(2,1)}, bf16[256,12800]{1,0:T(8,128)(2,1)S(1)}, u32[]{:S(2)}) copy-start(bf16[256,12800]{1,0:T(8,128)(2,1)S(1)} %get-tuple-element.12.right) | copy-start | bytes 19660804
  61.7 2.7 %copy-start.5 = (bf16[12800,256]{1,0:T(8,128)(2,1)}, bf16[12800,256]{1,0:T(8,128)(2,1)S(1)}, u32[]{:S(2)}) copy-start(bf16[12800,256]{1,0:T(8,128)(2,1)S(1)} %get-tuple-element.14.wcat) | copy-start | bytes 19660804
  64.4 4.6 %copy-start.2 = (bf16[24576,256]{1,0:T(8,128)(2,1)S(1)}, bf16[24576,256]{1,0:T(8,128)(2,1)}, u32[]{:S(2)}) copy-start(bf16[24576,256]{1,0:T(8,128)(2,1)} %copy-done.1) | copy-start | bytes 37748740
  69.0 2.9 %copy-start.4 = (bf16[256,12800]{1,0:T(8,128)(2,1)S(1)}, bf16[256,12800]{1,0:T(8,128)(2,1)}, u32[]{:S(2)}) copy-start(bf16[256,12800]{1,0:T(8,128)(2,1)} %copy-done.3) | copy-start | bytes 19660804
  71.8 2.9 %copy-start.6 = (bf16[12800,256]{1,0:T(8,128)(2,1)S(1)}, bf16[12800,256]{1,0:T(8,128)(2,1)}, u32[]{:S(2)}) copy-start(bf16[12800,256]{1,0:T(8,128)(2,1)} %copy-done.5) | copy-start | bytes 19660804
  74.7 0.8 copy-start.7

commit v3 on v2

--- a/solution.py
+++ b/solution.py
@@ -24,7 +24,7 @@
 SOURCES = 2 * COLPTS + 2 * SKEL
 CHUNK = 1024
 SCALE = LOG2E / 32.0
-K1_VMEM, K2_VMEM, K3_VMEM = 30 << 20, 8 << 20, 30 << 20
+K1_VMEM, K2_VMEM, K3_VMEM = 44 << 20, 24 << 20, 26 << 20
 CUTS = (0, 192, 384, 576, PAYLOAD)
 
 
@@ -100,9 +100,9 @@
 
 def gather_kernel(
     points_hbm, weights_hbm, proj_hbm, index, table,
-    left, right, norm, wcat, found,
-    payload, gathered, own, points, points2, weights, weights2, proj, coords, coords2, values, values2,
-    send, recv, pair_send, pair_recv, load_sem,
+    left_hbm, right, norm, wcat_hbm, found,
+    left, wcat, payload, gathered, own, points, points2, weights, weights2, proj, coords, coords2, values, values2,
+    send, recv, pair_send, pair_recv, load_sem, left_sem,
 ):
     y, z, x, core = place()
     loads = [
@@ -111,10 +111,15 @@
         ),
         pltpu.make_async_copy(points_hbm, points, load_sem.at[1]),
         pltpu.make_async_copy(weights_hbm, weights, load_sem.at[2]),
-        pltpu.make_async_copy(proj_hbm, proj, load_sem.at[3]),
     ]
+
+    def proj_load(n):
+        at = pl.multiple_of(n * CHUNK, CHUNK)
+        return pltpu.make_async_copy(proj_hbm.at[:, pl.ds(at, CHUNK)], proj.at[n % 2], load_sem.at[3 + n % 2])
+
     for c in loads:
         c.start()
+    proj_load(0).start()
     near = [(1, 0), (SIDE - 1, 0), (0, 1), (0, SIDE - 1)]
     peers = [device(y, (z + a) % SIDE, (x + b) % SIDE, core) for a, b in near]
     sibling = device(y, z, x, 1 - core)
@@ -127,7 +132,7 @@
         payload[leaf * HALF : (leaf + 1) * HALF, :] = packed.T
     payload[MINE * HALF :, :] = table[...]
 
-    started, swaps = [], []
+    started, swaps, handed = [], [], []
 
     def spot_of(k, i, j):
         az, ax = moved(k, z, x, -i, -j)
@@ -185,6 +190,10 @@
         lax.fori_loop(0, MINE, leaf_rows, 0)
         lists_here = payload[MINE * HALF :, :] if dz == dx == 0 else gathered[spot, MINE * HALF :, :]
         found[spot] = lists_here.astype(jnp.int32)
+        rows = pl.ds(pl.multiple_of(spot * (MINE * LEAF), LEAF), MINE * LEAF)
+        c = pltpu.make_async_copy(left.at[rows], left_hbm.at[rows], left_sem.at[dz * SIDE + dx])
+        c.start()
+        handed.append(c)
 
     def column(points_ref, weights_ref, base):
         def one(n, _):
@@ -212,14 +221,19 @@
     targets_at(0, 0)
     column(points, weights, 0)
     forward(1)
-    loads[3].wait()
     values[...] = jnp.zeros_like(values)
     coords[...] = jnp.zeros_like(coords)
 
     def skeleton(n, _):
+        proj_load(n).wait()
+
+        @pl.when(n + 1 < COLPTS // CHUNK)
+        def next_load():
+            proj_load(n + 1).start()
+
         at = pl.multiple_of(n * CHUNK, CHUNK)
         wh, wl = wcat[pl.ds(at, CHUNK), 0:WCOL], wcat[pl.ds(at, CHUNK), WCOL : 2 * WCOL]
-        ph, plow = split2(proj[:, pl.ds(at, CHUNK)])
+        ph, plow = split2(proj[n % 2])
         values[...] += mm(ph, wh) + mm(ph, wl) + mm(plow, wh)
         rows = lax.broadcasted_iota(jnp.int32, (CHUNK, SKEL), 0) + at
         pick = jnp.where(rows == index[...], 1.0, 0.0).astype(BF16)
@@ -243,6 +257,8 @@
     swaps[3].wait_recv()
     put_source(coords2[...], right, norm, 2 * COLPTS + SKEL)
     put_weights(values2[...], wcat, 2 * COLPTS + SKEL)
+    handed.append(pltpu.make_async_copy(wcat, wcat_hbm, load_sem.at[5]))
+    handed[-1].start()
     for level in (2, 3):
         for dz, dx in spots_of(level):
             targets_at(dz, dx)
@@ -252,23 +268,27 @@
             targets_at(dz, dx)
     for c in started + swaps:
         c.wait_send()
+    for c in handed:
+        c.wait()
 
 
 def gather(points, weights, proj, index, table):
-    anywhere = pl.BlockSpec(memory_space=pl.ANY)
+    hbm = pl.BlockSpec(memory_space=pltpu.HBM)
     vmem = pl.BlockSpec(memory_space=VMEM)
     return pl.pallas_call(
         gather_kernel,
         out_shape=(
-            pltpu.VMEM((TARGETS * LEAF, 256), BF16),
+            pltpu.HBM((TARGETS * LEAF, 256), BF16),
             pltpu.VMEM((4 * DIM, SOURCES), BF16),
             pltpu.VMEM((1, SOURCES), F32),
-            pltpu.VMEM((SOURCES, 2 * WCOL), BF16),
+            pltpu.HBM((SOURCES, 2 * WCOL), BF16),
             jax.ShapeDtypeStruct((SPOTS, 8, 128), jnp.int32),
         ),
-        in_specs=[anywhere] * 3 + [vmem] * 2,
-        out_specs=[vmem] * 5,
+        in_specs=[hbm] * 3 + [vmem] * 2,
+        out_specs=[hbm, vmem, vmem, hbm, vmem],
         scratch_shapes=[
+            VMEM((TARGETS * LEAF, 256), BF16),
+            VMEM((SOURCES, 2 * WCOL), BF16),
             VMEM((PAYLOAD, 128), F32),
             VMEM((SPOTS, PAYLOAD, 128), F32),
             VMEM((DIM, MINE * LEAF), F32),
@@ -276,7 +296,7 @@
             VMEM((DIM, COLPTS), F32),
             VMEM((COLPTS, WCOL), F32),
             VMEM((COLPTS, WCOL), F32),
-            VMEM((SKEL, COLPTS), F32),
+            VMEM((2, SKEL, CHUNK), F32),
             VMEM((DIM, SKEL), F32),
             VMEM((DIM, SKEL), F32),
             VMEM((SKEL, WCOL), F32),
@@ -285,7 +305,8 @@
             pltpu.SemaphoreType.DMA((4, 16)),
             pltpu.SemaphoreType.DMA((4,)),
             pltpu.SemaphoreType.DMA((4,)),
-            pltpu.SemaphoreType.DMA((4,)),
+            pltpu.SemaphoreType.DMA((6,)),
+            pltpu.SemaphoreType.DMA((SPOTS,)),
         ],
         compiler_params=pltpu.CompilerParams(
             collective_id=0, has_side_effects=True, vmem_limit_bytes=K1_VMEM
@@ -293,7 +314,17 @@
     )(points, weights, proj, index, table)
 
 
-def pair_kernel(spot_ref, table, left, right, norm, wcat, out, even, even_low, odd, odd_low, near_pairs, far_pairs):
+def pair_kernel(
+    spot_ref, table, left_hbm, right, norm, wcat_hbm, out,
+    even, even_low, odd, odd_low, left, wcat, near_pairs, far_pairs, sem,
+):
+    loads = [
+        pltpu.make_async_copy(wcat_hbm, wcat, sem.at[0]),
+        pltpu.make_async_copy(left_hbm, left, sem.at[1]),
+    ]
+    for c in loads:
+        c.start()
+
     def zero(t, _):
         out[pl.ds(pl.multiple_of(t * LEAF, LEAF), LEAF), :] = jnp.zeros((LEAF, WCOL), F32)
         return _
@@ -314,6 +345,8 @@
         return near, far
 
     near_count, far_count = lax.fori_loop(0, TARGETS, note, (0, 0))
+    for c in loads:
+        c.wait()
     for extra in range(3):
         near_pairs[near_count + extra] = TARGETS * 64
         far_pairs[far_count + extra] = TARGETS * 64
@@ -355,15 +388,19 @@
 def pairs(spot, table, left, right, norm, wcat):
     smem = pl.BlockSpec(memory_space=pltpu.SMEM)
     vmem = pl.BlockSpec(memory_space=VMEM)
+    hbm = pl.BlockSpec(memory_space=pltpu.HBM)
     return pl.pallas_call(
         pair_kernel,
         out_shape=pltpu.VMEM(((TARGETS + 1) * LEAF, WCOL), F32),
-        in_specs=[smem, smem] + [vmem] * 4,
+        in_specs=[smem, smem, hbm, vmem, vmem, hbm],
         out_specs=vmem,
         scratch_shapes=[VMEM((LEAF, LEAF), BF16)] * 4
         + [
+            VMEM((TARGETS * LEAF, 256), BF16),
+            VMEM((SOURCES, 2 * WCOL), BF16),
             pltpu.SMEM((TARGETS * 4 + 3,), jnp.int32),
             pltpu.SMEM((TARGETS * 2 + 3,), jnp.int32),
+            pltpu.SemaphoreType.DMA((2,)),
         ],
         compiler_params=pltpu.CompilerParams(vmem_limit_bytes=K2_VMEM),
     )(spot, table, left, right, norm, wcat)
@@ -529,9 +566,14 @@
 def on_device(points, weights, proj, fetch_table, near_list, far_list, skel_idx):
     y, z, x, core = place()
     table = lists(y, core, fetch_table, near_list, far_list)
+    fixed = pltpu.with_memory_space_constraint
+    points, weights, proj = (fixed(a, pltpu.HBM) for a in (points, weights, proj))
     left, right, norm, wcat, found = gather(points, weights, proj, skel_idx, table)
     spot = (z * SIDE + x).reshape(1).astype(jnp.int32)
-    partial = pairs(spot, found, left, right, norm, wcat)
+    partial = pairs(
+        spot, found, fixed(left, pltpu.HBM), fixed(right, VMEM), fixed(norm, VMEM), fixed(wcat, pltpu.HBM)
+    )
+    partial = fixed(partial, VMEM)
     return scatter(partial)
 
 

time: 209 us -> 192 us (0.919)
  local copies, waits for them, and re-layouts: 25.1 us -> 4.66 us
  Pallas kernels: 183 us -> 186 us
    unnamed x18 -> x6, local copies, waits for them, and re-layouts: 24.1 us -> 3.71 us
    pallas_call x1, Pallas kernels: 90.2 us -> 95.2 us  [scatter(): pl.pallas_call(scatter_kernel, out_shape=jax.ShapeDtypeStruct((COLPTS, WC...]
    pallas_call x1, Pallas kernels: 41.7 us -> 39.5 us  [pairs(): pl.pallas_call(pair_kernel, out_shape=pltpu.VMEM(((TARGETS + 1) * LEAF, W...]
where the time goes in v3:
time: 192 us; the launch traced here: 191 us
  Pallas kernels  186 us (97%)
  local copies, waits for them, and re-layouts  4.66 us (2%)
    pallas_call x1, Pallas kernels, scatter(): pl.pallas_call(scatter_kernel, out_shape=jax.ShapeDtypeStruct((COLPTS, WC...  95.2 us
    pallas_call x1, Pallas kernels, gather(): pl.pallas_call(gather_kernel, out_shape=(pltpu.HBM((TARGETS * LEAF, 256),...  51.5 us
    pallas_call x1, Pallas kernels, pairs(): pl.pallas_call(pair_kernel, out_shape=pltpu.VMEM(((TARGETS + 1) * LEAF, W...  39.5 us

profile of v3, /device:TPU:0, one launch (start us, length us, event | category | flops | bytes accessed | tf_op | source)
XLA Modules:
  0.0 191.4 jit_solution(7151170010898345251)
XLA Ops:
  0.0 0.0 copy-start
  0.0 0.1 iota_compare_fusion.2
  0.1 0.6 copy-done
  0.7 0.1 fusion
  0.8 0.8 constant_dynamic-slice_fusion
  1.6 0.1 copy.12
  1.6 0.1 fusion.1
  1.7 0.8 copy.11
  2.5 0.1 broadcast_in_dim.43
  2.6 0.1 select_reduce_fusion
  2.7 0.1 pad_add_fusion
  2.8 0.0 copy-start.1
  2.8 0.7 copy-done.1
  3.5 51.5 %shard_map.73 = (bf16[24576,256]{1,0:T(8,128)(2,1)}, bf16[256,12800]{1,0:T(8,128)(2,1)S(1)}, f32[1,12800]{1,0:T(1,128)S(1)}, bf16[12800,256]{1,0:T(8,128)(2,1)}, s32[16,8,128]{2,1,0:T(8,128)S(1)}) custom-call(f32[64,6144]{1,0:T(8,128)} %points_hbm.1, f32[6144,128]{1,0:T(8,128)} %weights_hbm.1, f32[256,6144]{1,0:T(8,128)} %proj_hbm.1, ...), custom_call_target="tpu_custom_call" | custom-call | tf_op jit(solution)/shard_map/pallas_call | solution.py:278
  55.0 39.5 %shard_map.74.partial = f32[25088,128]{1,0:T(8,128)S(1)} custom-call(s32[1]{0:T(128)} %bitcast.spot_ref, s32[16,8,128]{2,1,0:T(8,128)S(1)} %get-tuple-element.10.table, bf16[24576,256]{1,0:T(8,128)(2,1)} %get-tuple-element.11.left_hbm, bf16[256,12800]{1,0:T(8,128)(2,1)S(1)} %get-tuple-element.12.right, f32[1,12800]{1,0:T(1,128)S(1)} %get-tuple-element.13.norm, ...), custom_call_target="tpu_custom_call" | custom-call | tf_op jit(solution)/shard_map/pallas_call | solution.py:392
  94.5 95.2 %shard_map.75 = f32[6144,128]{1,0:T(8,128)S(1)} custom-call(f32[25088,128]{1,0:T(8,128)S(1)} %shard_map.74.partial), custom_call_target="tpu_custom_call" | custom-call | tf_op jit(solution)/shard_map/pallas_call | solution.py:528
  189.8 1.7 copy.14
  (8 shorter events, 0.1 us)
Async XLA Ops:
  0.0 0.7 copy-start
  2.8 0.7 copy-start.1

commit v4 on v3

--- a/solution.py
+++ b/solution.py
@@ -21,10 +21,14 @@
 HALF = LEAF // 2
 PAYLOAD = MINE * HALF + 8
 TARGETS = SPOTS * MINE
-SOURCES = 2 * COLPTS + 2 * SKEL
+IDLE = 2 * COLPTS + 2 * SKEL
+SOURCES = IDLE + LEAF
+BLOCK = 256
+BLOCKS = SOURCES // BLOCK
+LATER = (MINE - 1) * SPOTS
 CHUNK = 1024
 SCALE = LOG2E / 32.0
-K1_VMEM, K2_VMEM, K3_VMEM = 44 << 20, 24 << 20, 26 << 20
+K1_VMEM, K2_VMEM, K3_VMEM = 44 << 20, 33 << 20, 42 << 20
 CUTS = (0, 192, 384, 576, PAYLOAD)
 
 
@@ -63,20 +67,24 @@
     pl.semaphore_wait(barrier, len(peers))
 
 
-def put_source(block, right, norm, start):
-    width = block.shape[1]
+def put_source(block, right, norm, first):
     high, low = split2(block * (2.0 * SCALE))
-    right[0:DIM, pl.ds(start, width)] = high
-    right[DIM : 2 * DIM, pl.ds(start, width)] = high
-    right[2 * DIM : 3 * DIM, pl.ds(start, width)] = low
-    right[3 * DIM : 4 * DIM, pl.ds(start, width)] = jnp.full((DIM, width), -1.0, BF16)
-    norm[:, pl.ds(start, width)] = -SCALE * jnp.sum(block * block, axis=0, keepdims=True)
-
-
-def put_weights(block, wcat, start):
+    total = -SCALE * jnp.sum(block * block, axis=0, keepdims=True)
+    for n in range(block.shape[1] // BLOCK):
+        cols = slice(n * BLOCK, (n + 1) * BLOCK)
+        right[first + n, 0:DIM, :] = high[:, cols]
+        right[first + n, DIM : 2 * DIM, :] = high[:, cols]
+        right[first + n, 2 * DIM : 3 * DIM, :] = low[:, cols]
+        right[first + n, 3 * DIM : 4 * DIM, :] = jnp.full((DIM, BLOCK), -1.0, BF16)
+        norm[first + n] = total[:, cols]
+
+
+def put_weights(block, wcat, first):
     high, low = split2(block)
-    wcat[pl.ds(start, block.shape[0]), 0:WCOL] = high
-    wcat[pl.ds(start, block.shape[0]), WCOL : 2 * WCOL] = low
+    for n in range(block.shape[0] // BLOCK):
+        rows = slice(n * BLOCK, (n + 1) * BLOCK)
+        wcat[first + n, :, 0:WCOL] = high[rows]
+        wcat[first + n, :, WCOL : 2 * WCOL] = low[rows]
 
 
 def put_target(both, left, at):
@@ -184,22 +192,23 @@
         def leaf_rows(leaf, _):
             rows = pl.ds(pl.multiple_of(leaf * HALF, HALF), HALF)
             both = payload[rows, :] if dz == dx == 0 else gathered[spot, rows, :]
-            put_target(both, left, pl.multiple_of((spot * MINE + leaf) * LEAF, LEAF))
+            put_target(both, left, pl.multiple_of((leaf * SPOTS + spot) * LEAF, LEAF))
             return _
 
         lax.fori_loop(0, MINE, leaf_rows, 0)
         lists_here = payload[MINE * HALF :, :] if dz == dx == 0 else gathered[spot, MINE * HALF :, :]
         found[spot] = lists_here.astype(jnp.int32)
-        rows = pl.ds(pl.multiple_of(spot * (MINE * LEAF), LEAF), MINE * LEAF)
-        c = pltpu.make_async_copy(left.at[rows], left_hbm.at[rows], left_sem.at[dz * SIDE + dx])
-        c.start()
-        handed.append(c)
+        for leaf in range(MINE):
+            rows = pl.ds(pl.multiple_of((leaf * SPOTS + spot) * LEAF, LEAF), LEAF)
+            c = pltpu.make_async_copy(left.at[rows], left_hbm.at[rows], left_sem.at[leaf, dz * SIDE + dx])
+            c.start()
+            handed.append(c)
 
     def column(points_ref, weights_ref, base):
         def one(n, _):
             at = pl.multiple_of(n * LEAF, LEAF)
-            put_source(points_ref[:, pl.ds(at, LEAF)], right, norm, pl.multiple_of(base + at, LEAF))
-            put_weights(weights_ref[pl.ds(at, LEAF), :], wcat, pl.multiple_of(base + at, LEAF))
+            put_source(points_ref[:, pl.ds(at, LEAF)], right, norm, base + 2 * n)
+            put_weights(weights_ref[pl.ds(at, LEAF), :], wcat, base + 2 * n)
             return _
 
         lax.fori_loop(0, LEAVES, one, 0)
@@ -219,6 +228,10 @@
     swap(0, points, points2)
     swap(1, weights, weights2)
     targets_at(0, 0)
+    for n in range(IDLE // BLOCK, BLOCKS):
+        right[n] = jnp.zeros((4 * DIM, BLOCK), BF16)
+        norm[n] = jnp.zeros((1, BLOCK), F32)
+        wcat[n] = jnp.zeros((BLOCK, 2 * WCOL), BF16)
     column(points, weights, 0)
     forward(1)
     values[...] = jnp.zeros_like(values)
@@ -232,7 +245,8 @@
             proj_load(n + 1).start()
 
         at = pl.multiple_of(n * CHUNK, CHUNK)
-        wh, wl = wcat[pl.ds(at, CHUNK), 0:WCOL], wcat[pl.ds(at, CHUNK), WCOL : 2 * WCOL]
+        four = pl.ds(n * (CHUNK // BLOCK), CHUNK // BLOCK)
+        wh, wl = wcat[four, :, 0:WCOL].reshape(CHUNK, WCOL), wcat[four, :, WCOL : 2 * WCOL].reshape(CHUNK, WCOL)
         ph, plow = split2(proj[n % 2])
         values[...] += mm(ph, wh) + mm(ph, wl) + mm(plow, wh)
         rows = lax.broadcasted_iota(jnp.int32, (CHUNK, SKEL), 0) + at
@@ -247,16 +261,16 @@
     swap(2, coords, coords2)
     swap(3, values, values2)
     forward(2)
-    put_source(coords[...], right, norm, 2 * COLPTS)
-    put_weights(values[...], wcat, 2 * COLPTS)
+    put_source(coords[...], right, norm, 2 * COLPTS // BLOCK)
+    put_weights(values[...], wcat, 2 * COLPTS // BLOCK)
     swaps[0].wait_recv()
     swaps[1].wait_recv()
-    column(points2, weights2, COLPTS)
+    column(points2, weights2, COLPTS // BLOCK)
     forward(3)
     swaps[2].wait_recv()
     swaps[3].wait_recv()
-    put_source(coords2[...], right, norm, 2 * COLPTS + SKEL)
-    put_weights(values2[...], wcat, 2 * COLPTS + SKEL)
+    put_source(coords2[...], right, norm, (2 * COLPTS + SKEL) // BLOCK)
+    put_weights(values2[...], wcat, (2 * COLPTS + SKEL) // BLOCK)
     handed.append(pltpu.make_async_copy(wcat, wcat_hbm, load_sem.at[5]))
     handed[-1].start()
     for level in (2, 3):
@@ -279,16 +293,16 @@
         gather_kernel,
         out_shape=(
             pltpu.HBM((TARGETS * LEAF, 256), BF16),
-            pltpu.VMEM((4 * DIM, SOURCES), BF16),
-            pltpu.VMEM((1, SOURCES), F32),
-            pltpu.HBM((SOURCES, 2 * WCOL), BF16),
+            pltpu.VMEM((BLOCKS, 4 * DIM, BLOCK), BF16),
+            pltpu.VMEM((BLOCKS, 1, BLOCK), F32),
+            pltpu.HBM((BLOCKS, BLOCK, 2 * WCOL), BF16),
             jax.ShapeDtypeStruct((SPOTS, 8, 128), jnp.int32),
         ),
         in_specs=[hbm] * 3 + [vmem] * 2,
         out_specs=[hbm, vmem, vmem, hbm, vmem],
         scratch_shapes=[
             VMEM((TARGETS * LEAF, 256), BF16),
-            VMEM((SOURCES, 2 * WCOL), BF16),
+            VMEM((BLOCKS, BLOCK, 2 * WCOL), BF16),
             VMEM((PAYLOAD, 128), F32),
             VMEM((SPOTS, PAYLOAD, 128), F32),
             VMEM((DIM, MINE * LEAF), F32),
@@ -306,7 +320,7 @@
             pltpu.SemaphoreType.DMA((4,)),
             pltpu.SemaphoreType.DMA((4,)),
             pltpu.SemaphoreType.DMA((6,)),
-            pltpu.SemaphoreType.DMA((SPOTS,)),
+            pltpu.SemaphoreType.DMA((MINE, SPOTS)),
         ],
         compiler_params=pltpu.CompilerParams(
             collective_id=0, has_side_effects=True, vmem_limit_bytes=K1_VMEM
@@ -314,75 +328,134 @@
     )(points, weights, proj, index, table)
 
 
+def produce(left, right, norm, at, block, width, high_ref, low_ref):
+    blocks = range(width // BLOCK)
+    columns = jnp.concatenate([right[block + n] for n in blocks], axis=1)
+    norms = jnp.concatenate([norm[block + n] for n in blocks], axis=1)
+    power = mm(left[pl.ds(at, LEAF), :], columns) + norms
+    high_ref[:, :width], low_ref[:, :width] = split2(jnp.exp2(power))
+
+
+def consume(wcat, out, at, block, width, high_ref, low_ref):
+    rows = jnp.concatenate([wcat[block + n] for n in range(width // BLOCK)], axis=0)
+    total = mm(high_ref[:, :width], rows)
+    rest = mm(low_ref[:, :width], rows[:, :WCOL])
+    out[pl.ds(at, LEAF), :] += total[:, :WCOL] + total[:, WCOL:] + rest
+
+
+def near_start(source):
+    return source * (LEAF // BLOCK)
+
+
+def far_start(node):
+    return 2 * COLPTS // BLOCK + node
+
+
 def pair_kernel(
-    spot_ref, table, left_hbm, right, norm, wcat_hbm, out,
-    even, even_low, odd, odd_low, left, wcat, near_pairs, far_pairs, sem,
+    spot_ref, table, left_hbm, right, norm, wcat_hbm, out, extra_hbm, slots,
+    even, even_low, odd, odd_low, left, wcat, extra, near_pairs, far_pairs, near_extra, far_extra, sem,
 ):
+    first = pl.ds(0, SPOTS * LEAF)
+    later = pl.ds(SPOTS * LEAF, LATER * LEAF)
     loads = [
         pltpu.make_async_copy(wcat_hbm, wcat, sem.at[0]),
-        pltpu.make_async_copy(left_hbm, left, sem.at[1]),
+        pltpu.make_async_copy(left_hbm.at[later], left.at[later], sem.at[1]),
+        pltpu.make_async_copy(left_hbm.at[first], left.at[first], sem.at[2]),
     ]
     for c in loads:
         c.start()
 
-    def zero(t, _):
-        out[pl.ds(pl.multiple_of(t * LEAF, LEAF), LEAF), :] = jnp.zeros((LEAF, WCOL), F32)
-        return _
-
-    lax.fori_loop(0, TARGETS + 1, zero, 0)
+    def clear(ref, n):
+        def zero(t, _):
+            ref[pl.ds(pl.multiple_of(t * LEAF, LEAF), LEAF), :] = jnp.zeros((LEAF, WCOL), F32)
+            return _
+
+        lax.fori_loop(0, n, zero, 0)
+
+    clear(out, SPOTS + 1)
+    clear(extra, LATER + 1)
     spot = spot_ref[0]
+
+    def used(t, slot):
+        return table[t % SPOTS, t // SPOTS, slot]
 
     def note(t, counts):
         near, far = counts
         for slot in range(4):
-            source = table[t // MINE, t % MINE, 4 * spot + slot]
+            source = used(t, 4 * spot + slot)
             near_pairs[near] = t * 64 + source
             near = near + jnp.where(source >= 0, 1, 0)
         for slot in range(2):
-            node = table[t // MINE, t % MINE, 64 + 2 * spot + slot]
+            node = used(t, 64 + 2 * spot + slot)
             far_pairs[far] = t * 64 + node
             far = far + jnp.where(node >= 0, 1, 0)
         return near, far
 
-    near_count, far_count = lax.fori_loop(0, TARGETS, note, (0, 0))
-    for c in loads:
-        c.wait()
-    for extra in range(3):
-        near_pairs[near_count + extra] = TARGETS * 64
-        far_pairs[far_count + extra] = TARGETS * 64
-
-    def run(pair_list, count, base, width):
-        def columns(code):
-            return pl.ds(pl.multiple_of(base + (code % 64) * width, width), width)
-
-        def produce(n, high_ref, low_ref):
+    near_count, far_count = lax.fori_loop(0, SPOTS, note, (0, 0))
+
+    def note_later(t, counts):
+        near, far = counts
+        slots[t, 0], slots[t, 1], slots[t, 2] = IDLE // LEAF, IDLE // LEAF, 2
+        have = 0
+        for slot in range(4):
+            source = used(t + SPOTS, 4 * spot + slot)
+            hit = source >= 0
+            take = jnp.logical_and(hit, have < 2)
+            slots[t, jnp.where(take, have, 7)] = source
+            have = have + jnp.where(take, 1, 0)
+            near_extra[near] = t * 64 + source
+            near = near + jnp.where(jnp.logical_and(hit, jnp.logical_not(take)), 1, 0)
+        have = 0
+        for slot in range(2):
+            node = used(t + SPOTS, 64 + 2 * spot + slot)
+            hit = node >= 0
+            take = jnp.logical_and(hit, have < 1)
+            slots[t, jnp.where(take, 2, 7)] = node
+            have = have + jnp.where(take, 1, 0)
+            far_extra[far] = t * 64 + node
+            far = far + jnp.where(jnp.logical_and(hit, jnp.logical_not(take)), 1, 0)
+        return near, far
+
+    near_more, far_more = lax.fori_loop(0, LATER, note_later, (0, 0))
+    for n in range(3):
+        near_pairs[near_count + n] = SPOTS * 64
+        far_pairs[far_count + n] = SPOTS * 64
+        near_extra[near_more + n] = LATER * 64
+        far_extra[far_more + n] = LATER * 64
+
+    def run(pair_list, count, start_of, width, ref, n_targets, base):
+        def make(n, high_ref, low_ref):
             code = pair_list[n]
-            t, where = code // 64, columns(code)
-            at = pl.multiple_of(jnp.where(t < TARGETS, t, 0) * LEAF, LEAF)
-            power = mm(left[pl.ds(at, LEAF), :], right[:, where]) + norm[:, where]
-            high_ref[:, :width], low_ref[:, :width] = split2(jnp.exp2(power))
-
-        def consume(n, high_ref, low_ref):
+            t = code // 64
+            at = pl.multiple_of((base + jnp.where(t < n_targets, t, 0)) * LEAF, LEAF)
+            produce(left, right, norm, at, start_of(code % 64), width, high_ref, low_ref)
+
+        def use(n, high_ref, low_ref):
             code = pair_list[n]
-            t, where = code // 64, columns(code)
-            total = mm(high_ref[:, :width], wcat[where, :])
-            rest = mm(low_ref[:, :width], wcat[where, 0:WCOL])
-            at = pl.multiple_of(t * LEAF, LEAF)
-            out[pl.ds(at, LEAF), :] += total[:, :WCOL] + total[:, WCOL:] + rest
-
-        produce(0, even, even_low)
+            at = pl.multiple_of((code // 64) * LEAF, LEAF)
+            consume(wcat, ref, at, start_of(code % 64), width, high_ref, low_ref)
+
+        make(0, even, even_low)
 
         def two(m, _):
-            produce(2 * m + 1, odd, odd_low)
-            consume(2 * m, even, even_low)
-            produce(2 * m + 2, even, even_low)
-            consume(2 * m + 1, odd, odd_low)
+            make(2 * m + 1, odd, odd_low)
+            use(2 * m, even, even_low)
+            make(2 * m + 2, even, even_low)
+            use(2 * m + 1, odd, odd_low)
             return _
 
         lax.fori_loop(0, (count + 1) // 2, two, 0)
 
-    run(near_pairs, near_count, 0, LEAF)
-    run(far_pairs, far_count, 2 * COLPTS, SKEL)
+    loads[0].wait()
+    loads[1].wait()
+    run(near_extra, near_more, near_start, LEAF, extra, LATER, SPOTS)
+    run(far_extra, far_more, far_start, SKEL, extra, LATER, SPOTS)
+    handed = pltpu.make_async_copy(extra.at[pl.ds(0, LATER * LEAF)], extra_hbm, sem.at[3])
+    handed.start()
+    loads[2].wait()
+    run(near_pairs, near_count, near_start, LEAF, out, SPOTS, 0)
+    run(far_pairs, far_count, far_start, SKEL, out, SPOTS, 0)
+    handed.wait()
 
 
 def pairs(spot, table, left, right, norm, wcat):
@@ -391,16 +464,23 @@
     hbm = pl.BlockSpec(memory_space=pltpu.HBM)
     return pl.pallas_call(
         pair_kernel,
-        out_shape=pltpu.VMEM(((TARGETS + 1) * LEAF, WCOL), F32),
+        out_shape=(
+            pltpu.VMEM(((SPOTS + 1) * LEAF, WCOL), F32),
+            pltpu.HBM((LATER * LEAF, WCOL), F32),
+            jax.ShapeDtypeStruct((LATER, 8), jnp.int32),
+        ),
         in_specs=[smem, smem, hbm, vmem, vmem, hbm],
-        out_specs=vmem,
+        out_specs=(vmem, hbm, smem),
         scratch_shapes=[VMEM((LEAF, LEAF), BF16)] * 4
         + [
             VMEM((TARGETS * LEAF, 256), BF16),
-            VMEM((SOURCES, 2 * WCOL), BF16),
-            pltpu.SMEM((TARGETS * 4 + 3,), jnp.int32),
-            pltpu.SMEM((TARGETS * 2 + 3,), jnp.int32),
-            pltpu.SemaphoreType.DMA((2,)),
+            VMEM((BLOCKS, BLOCK, 2 * WCOL), BF16),
+            VMEM(((LATER + 1) * LEAF, WCOL), F32),
+            pltpu.SMEM((SPOTS * 4 + 3,), jnp.int32),
+            pltpu.SMEM((SPOTS * 2 + 3,), jnp.int32),
+            pltpu.SMEM((LATER * 4 + 3,), jnp.int32),
+            pltpu.SMEM((LATER * 2 + 3,), jnp.int32),
+            pltpu.SemaphoreType.DMA((4,)),
         ],
         compiler_params=pltpu.CompilerParams(vmem_limit_bytes=K2_VMEM),
     )(spot, table, left, right, norm, wcat)
@@ -409,8 +489,19 @@
 QUARTER = LEAF // 4
 
 
-def scatter_kernel(partial, out, slots, turn, send, recv, turn_send, turn_recv, y_send, y_recv):
+def scatter_kernel(
+    chosen, partial, extra_hbm, left_hbm, right, norm, wcat_hbm, out,
+    slots, turn, sums, left, wcat, even, even_low, odd, odd_low, third, third_low,
+    send, recv, turn_send, turn_recv, y_send, y_recv, load_sem,
+):
     y, z, x, core = place()
+    loads = [
+        pltpu.make_async_copy(left_hbm.at[pl.ds(SPOTS * LEAF, LATER * LEAF)], left, load_sem.at[0]),
+        pltpu.make_async_copy(wcat_hbm, wcat, load_sem.at[1]),
+        pltpu.make_async_copy(extra_hbm, sums, load_sem.at[2]),
+    ]
+    for c in loads:
+        c.start()
     near = [(1, 0), (SIDE - 1, 0), (0, 1), (0, SIDE - 1)]
     peers = [device(y, (z + a) % SIDE, (x + b) % SIDE, core) for a, b in near]
     above, below = device((y + 1) % SIDE, z, x, core), device((y + SIDE - 1) % SIDE, z, x, core)
@@ -419,45 +510,58 @@
 
     def own(k, leaf, first, second):
         az, ax = moved(k, z, x, first, second)
-        start = ((az * SIDE + ax) * MINE + leaf) * LEAF + k * QUARTER
-        return pl.ds(pl.multiple_of(start, QUARTER), QUARTER)
-
-    def begin(c):
-        c.start()
-        started.append(c)
+        place_of = az * SIDE + ax + (0 if leaf == 0 else (leaf - 1) * SPOTS)
+        rows = pl.ds(pl.multiple_of(place_of * LEAF + k * QUARTER, QUARTER), QUARTER)
+        return partial.at[rows] if leaf == 0 else sums.at[rows]
+
+    def begin(make):
+        make().start()
+        started.append(make)
 
     def step_first(k, leaf, step, j, source):
-        tz, tx = moved(k, z, x, 1, 0)
         n = (leaf * 3 + step) * SIDE + j
-        begin(pltpu.make_async_remote_copy(
-            src_ref=source, dst_ref=slots.at[k, n], send_sem=send.at[k, n], recv_sem=recv.at[k, n],
-            device_id=device(y, tz, tx, core), device_id_type=MESH,
-        ))
+
+        def make():
+            tz, tx = moved(k, z, x, 1, 0)
+            return pltpu.make_async_remote_copy(
+                src_ref=source(), dst_ref=slots.at[k, n], send_sem=send.at[k, n], recv_sem=recv.at[k, n],
+                device_id=device(y, tz, tx, core), device_id_type=MESH,
+            )
+
+        begin(make)
 
     def arrived_first(k, leaf, step, j):
         n = (leaf * 3 + step) * SIDE + j
         pltpu.make_async_copy(slots.at[k, n], slots.at[k, n], recv.at[k, n]).wait()
-        slots[k, n] += partial[own(k, leaf, 2 - step, 3 - j), :]
+        slots[k, n] += own(k, leaf, 2 - step, 3 - j)[...]
         return n
 
     def step_second(k, leaf, step, source):
-        tz, tx = moved(k, z, x, 0, 1)
         n = leaf * 3 + step
-        begin(pltpu.make_async_remote_copy(
-            src_ref=source, dst_ref=turn.at[k, n], send_sem=turn_send.at[k, n], recv_sem=turn_recv.at[k, n],
-            device_id=device(y, tz, tx, core), device_id_type=MESH,
-        ))
+
+        def make():
+            tz, tx = moved(k, z, x, 0, 1)
+            return pltpu.make_async_remote_copy(
+                src_ref=source(), dst_ref=turn.at[k, n], send_sem=turn_send.at[k, n], recv_sem=turn_recv.at[k, n],
+                device_id=device(y, tz, tx, core), device_id_type=MESH,
+            )
+
+        begin(make)
 
     def rows_of(plane, leaf, k):
         return pl.ds(pl.multiple_of((plane * MINE + leaf) * LEAF + k * QUARTER, QUARTER), QUARTER)
 
     def to_y(leaf, k, number, plane, up):
-        rows = rows_of(plane, leaf, k)
         n = (leaf * 4 + k) * 3 + number
-        begin(pltpu.make_async_remote_copy(
-            src_ref=out.at[rows], dst_ref=out.at[rows], send_sem=y_send.at[n], recv_sem=y_recv.at[n],
-            device_id=above if up else below, device_id_type=MESH,
-        ))
+
+        def make():
+            rows = rows_of(plane, leaf, k)
+            return pltpu.make_async_remote_copy(
+                src_ref=out.at[rows], dst_ref=out.at[rows], send_sem=y_send.at[n], recv_sem=y_recv.at[n],
+                device_id=above if up else below, device_id_type=MESH,
+            )
+
+        begin(make)
 
     def y_wait(leaf, k, number, plane):
         rows = rows_of(plane, leaf, k)
@@ -470,10 +574,10 @@
             m = leaf * 3 + j - 1
             pltpu.make_async_copy(turn.at[k, m], turn.at[k, m], turn_recv.at[k, m]).wait()
         if j == 0:
-            step_second(k, leaf, 0, slots.at[k, n])
+            step_second(k, leaf, 0, lambda: slots.at[k, n])
         elif j < 3:
             turn[k, m] += slots[k, n]
-            step_second(k, leaf, j, turn.at[k, m])
+            step_second(k, leaf, j, lambda: turn.at[k, m])
         else:
             out[rows_of(y, leaf, k), :] = turn[k, m] + slots[k, n]
             to_y(leaf, k, 0, y, True)
@@ -496,54 +600,100 @@
             y_wait(leaf, k, 0, lower)
         y_wait(leaf, k, 2, across)
 
+    def start_leaf(leaf):
+        for j in range(SIDE):
+            for k in range(4):
+                step_first(k, leaf, 0, j, functools.partial(own, k, leaf, 3, 3 - j))
+
+    def part(leaf, n):
+        j = n % SIDE
+        for k in range(4):
+            if leaf < MINE:
+                m = arrived_first(k, leaf, n // SIDE, j)
+                step_first(k, leaf, 1 + n // SIDE, j, lambda k=k, m=m: slots.at[k, m])
+            if leaf > 0 and n < SIDE:
+                second_axis(k, leaf - 1, j)
+
+    def make(t, slot, width, start_of, high_ref, low_ref):
+        at = pl.multiple_of(t * LEAF, LEAF)
+        produce(left, right, norm, at, start_of(chosen[t, slot]), width, high_ref, low_ref)
+
+    def use(t, slot, width, start_of, high_ref, low_ref):
+        at = pl.multiple_of(t * LEAF, LEAF)
+        consume(wcat, sums, at, start_of(chosen[t, slot]), width, high_ref, low_ref)
+
+    def one_target(t):
+        make(t, 1, LEAF, near_start, odd, odd_low)
+        use(t, 0, LEAF, near_start, even, even_low)
+        make(t, 2, SKEL, far_start, third, third_low)
+        use(t, 1, LEAF, near_start, odd, odd_low)
+        make((t + 1) % LATER, 0, LEAF, near_start, even, even_low)
+        use(t, 2, SKEL, far_start, third, third_low)
+
     for leaf in range(MINE + 1):
         if leaf < MINE:
-            for j in range(SIDE):
-                for k in range(4):
-                    step_first(k, leaf, 0, j, partial.at[own(k, leaf, 3, 3 - j)])
-        for j in range(SIDE):
-            for k in range(4):
-                if leaf < MINE:
-                    n = arrived_first(k, leaf, 0, j)
-                    step_first(k, leaf, 1, j, slots.at[k, n])
-                if leaf > 0:
-                    second_axis(k, leaf - 1, j)
-        if leaf < MINE:
-            for j in range(SIDE):
-                for k in range(4):
-                    n = arrived_first(k, leaf, 1, j)
-                    step_first(k, leaf, 2, j, slots.at[k, n])
+            start_leaf(leaf)
+        if leaf == 0:
+            for c in loads:
+                c.wait()
+            make(0, 0, LEAF, near_start, even, even_low)
+        if leaf < MINE - 1:
+
+            def step(n, _, leaf=leaf):
+                def inner(m, carry):
+                    one_target(leaf * SPOTS + 2 * n + m)
+                    return carry
+
+                lax.fori_loop(0, 2, inner, 0)
+                for which in range(2 * SIDE):
+                    pl.when(n == which)(functools.partial(part, leaf, which))
+                return _
+
+            lax.fori_loop(0, 2 * SIDE, step, 0)
+        else:
+            for n in range(2 * SIDE):
+                part(leaf, n)
         if leaf > 0:
             for k in range(4):
                 second_hop(leaf - 1, k)
     for leaf in range(MINE):
         for k in range(4):
             last_arrivals(leaf, k)
-    for c in started:
-        c.wait_send()
-
-
-def scatter(partial):
+    for again in started:
+        again().wait_send()
+
+
+def scatter(chosen, partial, extra, left, right, norm, wcat):
+    smem = pl.BlockSpec(memory_space=pltpu.SMEM)
     vmem = pl.BlockSpec(memory_space=VMEM)
+    hbm = pl.BlockSpec(memory_space=pltpu.HBM)
     return pl.pallas_call(
         scatter_kernel,
         out_shape=jax.ShapeDtypeStruct((COLPTS, WCOL), F32),
-        in_specs=[vmem],
+        in_specs=[smem, vmem, hbm, hbm, vmem, vmem, hbm],
         out_specs=vmem,
         scratch_shapes=[
             VMEM((4, MINE * 3 * SIDE, QUARTER, WCOL), F32),
             VMEM((4, MINE * 3, QUARTER, WCOL), F32),
+            VMEM((LATER * LEAF, WCOL), F32),
+            VMEM((LATER * LEAF, 256), BF16),
+            VMEM((BLOCKS, BLOCK, 2 * WCOL), BF16),
+        ]
+        + [VMEM((LEAF, LEAF), BF16)] * 4
+        + [VMEM((LEAF, SKEL), BF16)] * 2
+        + [
             pltpu.SemaphoreType.DMA((4, MINE * 3 * SIDE)),
             pltpu.SemaphoreType.DMA((4, MINE * 3 * SIDE)),
             pltpu.SemaphoreType.DMA((4, MINE * 3)),
             pltpu.SemaphoreType.DMA((4, MINE * 3)),
             pltpu.SemaphoreType.DMA((MINE * 4 * 3,)),
             pltpu.SemaphoreType.DMA((MINE * 4 * 3,)),
+            pltpu.SemaphoreType.DMA((3,)),
         ],
         compiler_params=pltpu.CompilerParams(
             collective_id=1, has_side_effects=True, vmem_limit_bytes=K3_VMEM
         ),
-    )(partial)
+    )(chosen, partial, extra, left, right, norm, wcat)
 
 
 def lists(y, core, fetch_table, near_list, far_list):
@@ -570,11 +720,10 @@
     points, weights, proj = (fixed(a, pltpu.HBM) for a in (points, weights, proj))
     left, right, norm, wcat, found = gather(points, weights, proj, skel_idx, table)
     spot = (z * SIDE + x).reshape(1).astype(jnp.int32)
-    partial = pairs(
-        spot, found, fixed(left, pltpu.HBM), fixed(right, VMEM), fixed(norm, VMEM), fixed(wcat, pltpu.HBM)
-    )
-    partial = fixed(partial, VMEM)
-    return scatter(partial)
+    left, wcat = fixed(left, pltpu.HBM), fixed(wcat, pltpu.HBM)
+    right, norm = fixed(right, VMEM), fixed(norm, VMEM)
+    partial, extra, chosen = pairs(spot, found, left, right, norm, wcat)
+    return scatter(chosen, fixed(partial, VMEM), fixed(extra, pltpu.HBM), left, right, norm, wcat)
 
 
 def solution(mesh):

time: 192 us -> 192 us (level)
  local copies, waits for them, and re-layouts: 4.66 us -> 6.75 us
    pallas_call x1, Pallas kernels: 39.5 us -> 20 us  [pairs(): pl.pallas_call(pair_kernel, out_shape=(pltpu.VMEM(((SPOTS + 1) * LEAF, WC...]
    pallas_call x1, Pallas kernels: 95.2 us -> 113 us  [scatter(): pl.pallas_call(scatter_kernel, out_shape=jax.ShapeDtypeStruct((COLPTS, WC...]
    unnamed x6, local copies, waits for them, and re-layouts: 3.71 us -> 5.8 us
where the time goes in v4:
time: 192 us
  Pallas kernels  185 us (96%)
  local copies, waits for them, and re-layouts  6.75 us (4%)
    pallas_call x1, Pallas kernels, scatter(): pl.pallas_call(scatter_kernel, out_shape=jax.ShapeDtypeStruct((COLPTS, WC...  113 us
    pallas_call x1, Pallas kernels, gather(): pl.pallas_call(gather_kernel, out_shape=(pltpu.HBM((TARGETS * LEAF, 256),...  51.8 us
    pallas_call x1, Pallas kernels, pairs(): pl.pallas_call(pair_kernel, out_shape=(pltpu.VMEM(((SPOTS + 1) * LEAF, WC...  20 us
    unnamed x6, local copies, waits for them, and re-layouts  5.8 us

profile of v4, /device:TPU:0, one launch (start us, length us, event | category | flops | bytes accessed | tf_op | source)
XLA Modules:
  0.0 191.9 jit_solution(7252803308599081620)
XLA Ops:
  0.0 0.0 copy-start
  0.0 0.1 iota_compare_fusion.2
  0.1 0.6 copy-done
  0.7 0.1 fusion
  0.8 0.8 constant_dynamic-slice_fusion
  1.6 0.1 copy.12
  1.6 0.1 fusion.1
  1.7 0.8 copy.11
  2.5 0.1 broadcast_in_dim.43
  2.6 0.1 select_reduce_fusion
  2.7 0.1 pad_add_fusion
  2.8 0.0 copy-start.1
  2.8 0.7 copy-done.1
  3.5 51.8 %shard_map.73 = (bf16[24576,256]{1,0:T(8,128)(2,1)}, bf16[52,256,256]{2,1,0:T(8,128)(2,1)S(1)}, f32[52,1,256]{2,1,0:T(1,128)S(1)}, bf16[52,256,256]{2,1,0:T(8,128)(2,1)}, s32[16,8,128]{2,1,0:T(8,128)S(1)}) custom-call(f32[64,6144]{1,0:T(8,128)} %points_hbm.1, f32[6144,128]{1,0:T(8,128)} %weights_hbm.1, f32[256,6144]{1,0:T(8,128)} %proj_hbm.1, ...), custom_call_target="tpu_custom_call" | custom-call | tf_op jit(solution)/shard_map/pallas_call | solution.py:292
  55.4 20.0 %shard_map.74 = (f32[8704,128]{1,0:T(8,128)S(1)}, f32[16384,128]{1,0:T(8,128)}, s32[32,8]{1,0:T(8,128)S(1)}) custom-call(s32[1]{0:T(128)} %bitcast.spot_ref, s32[16,8,128]{2,1,0:T(8,128)S(1)} %get-tuple-element.13.table, bf16[24576,256]{1,0:T(8,128)(2,1)} %get-tuple-element.14.left_hbm, bf16[52,256,256]{2,1,0:T(8,128)(2,1)S(1)} %get-tuple-element.15.right, ...), custom_call_target="tpu_custom_call" | custom-call | tf_op jit(solution)/shard_map/pallas_call | solution.py:465
  75.3 112.8 %shard_map.75 = f32[6144,128]{1,0:T(8,128)} custom-call(s32[32,8]{1,0:T(8,128)S(1)} %get-tuple-element.18.chosen, f32[8704,128]{1,0:T(8,128)S(1)} %get-tuple-element.19.partial, f32[16384,128]{1,0:T(8,128)} %get-tuple-element.20.extra_hbm, bf16[24576,256]{1,0:T(8,128)(2,1)} %get-tuple-element.14.left_hbm, bf16[52,256,256]{2,1,0:T(8,128)(2,1)S(1)} %get-tuple-element.15.right, ...), custom_call_target="tpu_custom_call" | custom-call | tf_op jit(solution)/shard_map/pallas_call | solution.py:670
  188.1 3.8 %copy.14 = f32[6144,128]{1,0:T(8,128)} copy(f32[6144,128]{1,0:T(8,128)} %shard_map.75) | data formatting | bytes 6291456
  (8 shorter events, 0.1 us)
Async XLA Ops:
  0.0 0.7 copy-start
  2.8 0.7 copy-start.1

commit v5 on v4

--- a/solution.py
+++ b/solution.py
@@ -28,7 +28,7 @@
 LATER = (MINE - 1) * SPOTS
 CHUNK = 1024
 SCALE = LOG2E / 32.0
-K1_VMEM, K2_VMEM, K3_VMEM = 44 << 20, 33 << 20, 42 << 20
+K1_VMEM, K2_VMEM, K3_VMEM = 44 << 20, 32 << 20, 38 << 20
 CUTS = (0, 192, 384, 576, PAYLOAD)
 
 
@@ -395,13 +395,13 @@
 
     def note_later(t, counts):
         near, far = counts
-        slots[t, 0], slots[t, 1], slots[t, 2] = IDLE // LEAF, IDLE // LEAF, 2
+        slots[t, 0], slots[t, 1] = IDLE // LEAF, 2
         have = 0
         for slot in range(4):
             source = used(t + SPOTS, 4 * spot + slot)
             hit = source >= 0
-            take = jnp.logical_and(hit, have < 2)
-            slots[t, jnp.where(take, have, 7)] = source
+            take = jnp.logical_and(hit, have < 1)
+            slots[t, jnp.where(take, 0, 7)] = source
             have = have + jnp.where(take, 1, 0)
             near_extra[near] = t * 64 + source
             near = near + jnp.where(jnp.logical_and(hit, jnp.logical_not(take)), 1, 0)
@@ -410,7 +410,7 @@
             node = used(t + SPOTS, 64 + 2 * spot + slot)
             hit = node >= 0
             take = jnp.logical_and(hit, have < 1)
-            slots[t, jnp.where(take, 2, 7)] = node
+            slots[t, jnp.where(take, 1, 7)] = node
             have = have + jnp.where(take, 1, 0)
             far_extra[far] = t * 64 + node
             far = far + jnp.where(jnp.logical_and(hit, jnp.logical_not(take)), 1, 0)
@@ -491,7 +491,7 @@
 
 def scatter_kernel(
     chosen, partial, extra_hbm, left_hbm, right, norm, wcat_hbm, out,
-    slots, turn, sums, left, wcat, even, even_low, odd, odd_low, third, third_low,
+    slots, turn, sums, left, wcat, even, even_low, odd, odd_low,
     send, recv, turn_send, turn_recv, y_send, y_recv, load_sem,
 ):
     y, z, x, core = place()
@@ -623,12 +623,10 @@
         consume(wcat, sums, at, start_of(chosen[t, slot]), width, high_ref, low_ref)
 
     def one_target(t):
-        make(t, 1, LEAF, near_start, odd, odd_low)
+        make(t, 1, SKEL, far_start, odd, odd_low)
         use(t, 0, LEAF, near_start, even, even_low)
-        make(t, 2, SKEL, far_start, third, third_low)
-        use(t, 1, LEAF, near_start, odd, odd_low)
         make((t + 1) % LATER, 0, LEAF, near_start, even, even_low)
-        use(t, 2, SKEL, far_start, third, third_low)
+        use(t, 1, SKEL, far_start, odd, odd_low)
 
     for leaf in range(MINE + 1):
         if leaf < MINE:
@@ -679,7 +677,7 @@
             VMEM((LATER * LEAF, 256), BF16),
             VMEM((BLOCKS, BLOCK, 2 * WCOL), BF16),
         ]
-        + [VMEM((LEAF, LEAF), BF16)] * 4
+        + [VMEM((LEAF, LEAF), BF16)] * 2
         + [VMEM((LEAF, SKEL), BF16)] * 2
         + [
             pltpu.SemaphoreType.DMA((4, MINE * 3 * SIDE)),

time: 192 us -> 183 us (0.953)
  Pallas kernels: 185 us -> 178 us
  local copies, waits for them, and re-layouts: 6.75 us -> 4.66 us
    pallas_call x1, Pallas kernels: 113 us -> 97.5 us  [scatter(): pl.pallas_call(scatter_kernel, out_shape=jax.ShapeDtypeStruct((COLPTS, WC...]
    pallas_call x1, Pallas kernels: 20 us -> 28.4 us  [pairs(): pl.pallas_call(pair_kernel, out_shape=(pltpu.VMEM(((SPOTS + 1) * LEAF, WC...]
    unnamed x6, local copies, waits for them, and re-layouts: 5.8 us -> 3.71 us
where the time goes in v5:
time: 183 us
  Pallas kernels  178 us (97%)
  local copies, waits for them, and re-layouts  4.66 us (3%)
    pallas_call x1, Pallas kernels, scatter(): pl.pallas_call(scatter_kernel, out_shape=jax.ShapeDtypeStruct((COLPTS, WC...  97.5 us
    pallas_call x1, Pallas kernels, gather(): pl.pallas_call(gather_kernel, out_shape=(pltpu.HBM((TARGETS * LEAF, 256),...  51.8 us
    pallas_call x1, Pallas kernels, pairs(): pl.pallas_call(pair_kernel, out_shape=(pltpu.VMEM(((SPOTS + 1) * LEAF, WC...  28.4 us
    unnamed x6, local copies, waits for them, and re-layouts  3.71 us

profile of v5, /device:TPU:0, one launch (start us, length us, event | category | flops | bytes accessed | tf_op | source)
XLA Modules:
  0.0 182.9 jit_solution(6596427164846263966)
XLA Ops:
  0.0 0.0 copy-start
  0.0 0.1 iota_compare_fusion.2
  0.1 0.6 copy-done
  0.7 0.1 fusion
  0.8 0.8 constant_dynamic-slice_fusion
  1.6 0.1 copy.12
  1.6 0.1 fusion.1
  1.7 0.8 copy.11
  2.5 0.1 broadcast_in_dim.43
  2.6 0.1 select_reduce_fusion
  2.7 0.1 pad_add_fusion
  2.8 0.0 copy-start.1
  2.8 0.7 copy-done.1
  3.5 51.8 %shard_map.73 = (bf16[24576,256]{1,0:T(8,128)(2,1)}, bf16[52,256,256]{2,1,0:T(8,128)(2,1)S(1)}, f32[52,1,256]{2,1,0:T(1,128)S(1)}, bf16[52,256,256]{2,1,0:T(8,128)(2,1)}, s32[16,8,128]{2,1,0:T(8,128)S(1)}) custom-call(f32[64,6144]{1,0:T(8,128)} %points_hbm.1, f32[6144,128]{1,0:T(8,128)} %weights_hbm.1, f32[256,6144]{1,0:T(8,128)} %proj_hbm.1, ...), custom_call_target="tpu_custom_call" | custom-call | tf_op jit(solution)/shard_map/pallas_call | solution.py:292
  55.3 28.4 %shard_map.74 = (f32[8704,128]{1,0:T(8,128)S(1)}, f32[16384,128]{1,0:T(8,128)}, s32[32,8]{1,0:T(8,128)S(1)}) custom-call(s32[1]{0:T(128)} %bitcast.spot_ref, s32[16,8,128]{2,1,0:T(8,128)S(1)} %get-tuple-element.13.table, bf16[24576,256]{1,0:T(8,128)(2,1)} %get-tuple-element.14.left_hbm, bf16[52,256,256]{2,1,0:T(8,128)(2,1)S(1)} %get-tuple-element.15.right, ...), custom_call_target="tpu_custom_call" | custom-call | tf_op jit(solution)/shard_map/pallas_call | solution.py:465
  83.8 97.5 %shard_map.75 = f32[6144,128]{1,0:T(8,128)S(1)} custom-call(s32[32,8]{1,0:T(8,128)S(1)} %get-tuple-element.18.chosen, f32[8704,128]{1,0:T(8,128)S(1)} %get-tuple-element.19.partial, f32[16384,128]{1,0:T(8,128)} %get-tuple-element.20.extra_hbm, bf16[24576,256]{1,0:T(8,128)(2,1)} %get-tuple-element.14.left_hbm, ...), custom_call_target="tpu_custom_call" | custom-call | tf_op jit(solution)/shard_map/pallas_call | solution.py:668
  181.2 1.7 copy.14
  (8 shorter events, 0.1 us)
Async XLA Ops:
  0.0 0.7 copy-start
  2.8 0.7 copy-start.1

commit v6 on v5

--- a/solution.py
+++ b/solution.py
@@ -43,21 +43,31 @@
 
 def place():
     y, dev = lax.axis_index("grp"), lax.axis_index("dev")
-    return y, dev // 8, (dev // 2) % SIDE, dev % 2
-
-
-def device(y, z, x, core):
-    return (y, (z * SIDE + x) * 2 + core)
-
-
-def stream_axes(k):
-    return k < 2, 1 if k % 2 == 0 else SIDE - 1
-
-
-def moved(k, z, x, first, second):
-    x_first, sign = stream_axes(k)
-    along_x, along_z = (first, second) if x_first else (second, first)
-    return (z + sign * along_z) % SIDE, (x + sign * along_x) % SIDE
+    return y, lax.div(dev, 8), lax.rem(lax.div(dev, 2), SIDE), lax.rem(dev, 2)
+
+
+def shift(k, first, second):
+    sign = 1 if k % 2 == 0 else -1
+    along_x, along_z = (first, second) if k < 2 else (second, first)
+    return sign * along_z % SIDE, sign * along_x % SIDE
+
+
+class Around:
+    def __init__(self):
+        self.y, self.z, self.x, self.core = place()
+        zs = [lax.rem(self.z + a, SIDE) for a in range(SIDE)]
+        xs = [lax.rem(self.x + a, SIDE) for a in range(SIDE)]
+        self.spots = {(a, b): zs[a] * SIDE + xs[b] for a in range(SIDE) for b in range(SIDE)}
+        self.devices = {
+            (a, b): (self.y, self.spots[a, b] * 2 + self.core) for a, b in ((1, 0), (3, 0), (0, 1), (0, 3))
+        }
+        self.sibling = (self.y, self.spots[0, 0] * 2 + 1 - self.core)
+
+    def spot(self, k, first, second):
+        return self.spots[shift(k, first, second)]
+
+    def next(self, k, along_first):
+        return self.devices[shift(k, 1, 0) if along_first else shift(k, 0, 1)]
 
 
 def greet(peers):
@@ -112,7 +122,8 @@
     left, wcat, payload, gathered, own, points, points2, weights, weights2, proj, coords, coords2, values, values2,
     send, recv, pair_send, pair_recv, load_sem, left_sem,
 ):
-    y, z, x, core = place()
+    around = Around()
+    y = around.y
     loads = [
         pltpu.make_async_copy(
             points_hbm.at[:, pl.ds(pl.multiple_of(y * (MINE * LEAF), LEAF), MINE * LEAF)], own, load_sem.at[0]
@@ -128,10 +139,7 @@
     for c in loads:
         c.start()
     proj_load(0).start()
-    near = [(1, 0), (SIDE - 1, 0), (0, 1), (0, SIDE - 1)]
-    peers = [device(y, (z + a) % SIDE, (x + b) % SIDE, core) for a, b in near]
-    sibling = device(y, z, x, 1 - core)
-    greet(peers + [sibling])
+    greet(list(around.devices.values()) + [around.sibling])
 
     loads[0].wait()
     for leaf in range(MINE):
@@ -143,12 +151,10 @@
     started, swaps, handed = [], [], []
 
     def spot_of(k, i, j):
-        az, ax = moved(k, z, x, -i, -j)
-        return az * SIDE + ax
+        return around.spot(k, -i, -j)
 
     def copy(k, i, j, first):
         rows = pl.ds(CUTS[k], CUTS[k + 1] - CUTS[k])
-        tz, tx = moved(k, z, x, 1 if first else 0, 0 if first else 1)
         arrival = (i + 1) * SIDE + j if first else i * SIDE + j + 1
         number = i if first else SIDE - 1 + i * (SIDE - 1) + j
         target = gathered.at[spot_of(k, i, j), rows]
@@ -157,7 +163,7 @@
             dst_ref=target,
             send_sem=send.at[k, number],
             recv_sem=recv.at[k, arrival],
-            device_id=device(y, tz, tx, core),
+            device_id=around.next(k, first),
             device_id_type=MESH,
         )
         c.start()
@@ -181,13 +187,13 @@
     def swap(n, a, b):
         c = pltpu.make_async_remote_copy(
             src_ref=a, dst_ref=b, send_sem=pair_send.at[n], recv_sem=pair_recv.at[n],
-            device_id=sibling, device_id_type=MESH,
+            device_id=around.sibling, device_id_type=MESH,
         )
         c.start()
         swaps.append(c)
 
     def targets_at(dz, dx):
-        spot = (z + dz) % SIDE * SIDE + (x + dx) % SIDE
+        spot = around.spots[dz, dx]
 
         def leaf_rows(leaf, _):
             rows = pl.ds(pl.multiple_of(leaf * HALF, HALF), HALF)
@@ -494,7 +500,8 @@
     slots, turn, sums, left, wcat, even, even_low, odd, odd_low,
     send, recv, turn_send, turn_recv, y_send, y_recv, load_sem,
 ):
-    y, z, x, core = place()
+    around = Around()
+    y = around.y
     loads = [
         pltpu.make_async_copy(left_hbm.at[pl.ds(SPOTS * LEAF, LATER * LEAF)], left, load_sem.at[0]),
         pltpu.make_async_copy(wcat_hbm, wcat, load_sem.at[1]),
@@ -502,15 +509,14 @@
     ]
     for c in loads:
         c.start()
-    near = [(1, 0), (SIDE - 1, 0), (0, 1), (0, SIDE - 1)]
-    peers = [device(y, (z + a) % SIDE, (x + b) % SIDE, core) for a, b in near]
-    above, below = device((y + 1) % SIDE, z, x, core), device((y + SIDE - 1) % SIDE, z, x, core)
-    greet(peers + [above, below])
+    planes = [lax.rem(y + a, SIDE) for a in range(SIDE)]
+    here = around.spots[0, 0] * 2 + around.core
+    above, below = (planes[1], here), (planes[3], here)
+    greet(list(around.devices.values()) + [above, below])
     started = []
 
     def own(k, leaf, first, second):
-        az, ax = moved(k, z, x, first, second)
-        place_of = az * SIDE + ax + (0 if leaf == 0 else (leaf - 1) * SPOTS)
+        place_of = around.spot(k, first, second) + (0 if leaf == 0 else (leaf - 1) * SPOTS)
         rows = pl.ds(pl.multiple_of(place_of * LEAF + k * QUARTER, QUARTER), QUARTER)
         return partial.at[rows] if leaf == 0 else sums.at[rows]
 
@@ -522,10 +528,9 @@
         n = (leaf * 3 + step) * SIDE + j
 
         def make():
-            tz, tx = moved(k, z, x, 1, 0)
             return pltpu.make_async_remote_copy(
                 src_ref=source(), dst_ref=slots.at[k, n], send_sem=send.at[k, n], recv_sem=recv.at[k, n],
-                device_id=device(y, tz, tx, core), device_id_type=MESH,
+                device_id=around.next(k, True), device_id_type=MESH,
             )
 
         begin(make)
@@ -540,10 +545,9 @@
         n = leaf * 3 + step
 
         def make():
-            tz, tx = moved(k, z, x, 0, 1)
             return pltpu.make_async_remote_copy(
                 src_ref=source(), dst_ref=turn.at[k, n], send_sem=turn_send.at[k, n], recv_sem=turn_recv.at[k, n],
-                device_id=device(y, tz, tx, core), device_id_type=MESH,
+                device_id=around.next(k, False), device_id_type=MESH,
             )
 
         begin(make)
@@ -584,7 +588,7 @@
             to_y(leaf, k, 1, y, False)
 
     def second_hop(leaf, k):
-        lower, upper = (y + SIDE - 1) % SIDE, (y + 1) % SIDE
+        lower, upper = planes[3], planes[1]
         if k % 2 == 0:
             y_wait(leaf, k, 0, lower)
             to_y(leaf, k, 2, lower, True)
@@ -593,7 +597,7 @@
             to_y(leaf, k, 2, upper, False)
 
     def last_arrivals(leaf, k):
-        lower, upper, across = (y + SIDE - 1) % SIDE, (y + 1) % SIDE, (y + 2) % SIDE
+        lower, upper, across = planes[3], planes[1], planes[2]
         if k % 2 == 0:
             y_wait(leaf, k, 1, upper)
         else:

time: 183 us -> 184 us (level)
    pallas_call x1, Pallas kernels: 97.5 us -> 101 us  [scatter(): pl.pallas_call(scatter_kernel, out_shape=jax.ShapeDtypeStruct((COLPTS, WC...]
    pallas_call x1, Pallas kernels: 28.4 us -> 25 us  [pairs(): pl.pallas_call(pair_kernel, out_shape=(pltpu.VMEM(((SPOTS + 1) * LEAF, WC...]
where the time goes in v6:
time: 184 us; the launch traced here: 183 us
  Pallas kernels  178 us (97%)
  local copies, waits for them, and re-layouts  4.66 us (3%)
    pallas_call x1, Pallas kernels, scatter(): pl.pallas_call(scatter_kernel, out_shape=jax.ShapeDtypeStruct((COLPTS, WC...  101 us
    pallas_call x1, Pallas kernels, gather(): pl.pallas_call(gather_kernel, out_shape=(pltpu.HBM((TARGETS * LEAF, 256),...  51.9 us
    pallas_call x1, Pallas kernels, pairs(): pl.pallas_call(pair_kernel, out_shape=(pltpu.VMEM(((SPOTS + 1) * LEAF, WC...  25 us
    unnamed x6, local copies, waits for them, and re-layouts  3.71 us

profile of v6, /device:TPU:0, one launch (start us, length us, event | category | flops | bytes accessed | tf_op | source)
XLA Modules:
  0.0 183.5 jit_solution(11838249400178982629)
XLA Ops:
  0.0 0.0 copy-start
  0.0 0.1 iota_compare_fusion.2
  0.1 0.6 copy-done
  0.7 0.1 fusion
  0.8 0.8 constant_dynamic-slice_fusion
  1.6 0.1 copy.12
  1.6 0.1 fusion.1
  1.7 0.8 copy.11
  2.5 0.1 broadcast_in_dim.43
  2.6 0.1 select_reduce_fusion
  2.7 0.1 pad_add_fusion
  2.8 0.0 copy-start.1
  2.8 0.7 copy-done.1
  3.5 51.9 %shard_map.73 = (bf16[24576,256]{1,0:T(8,128)(2,1)}, bf16[52,256,256]{2,1,0:T(8,128)(2,1)S(1)}, f32[52,1,256]{2,1,0:T(1,128)S(1)}, bf16[52,256,256]{2,1,0:T(8,128)(2,1)}, s32[16,8,128]{2,1,0:T(8,128)S(1)}) custom-call(f32[64,6144]{1,0:T(8,128)} %points_hbm.1, f32[6144,128]{1,0:T(8,128)} %weights_hbm.1, f32[256,6144]{1,0:T(8,128)} %proj_hbm.1, ...), custom_call_target="tpu_custom_call" | custom-call | tf_op jit(solution)/shard_map/pallas_call | solution.py:298
  55.4 25.0 %shard_map.74 = (f32[8704,128]{1,0:T(8,128)S(1)}, f32[16384,128]{1,0:T(8,128)}, s32[32,8]{1,0:T(8,128)S(1)}) custom-call(s32[1]{0:T(128)} %bitcast.spot_ref, s32[16,8,128]{2,1,0:T(8,128)S(1)} %get-tuple-element.13.table, bf16[24576,256]{1,0:T(8,128)(2,1)} %get-tuple-element.14.left_hbm, bf16[52,256,256]{2,1,0:T(8,128)(2,1)S(1)} %get-tuple-element.15.right, ...), custom_call_target="tpu_custom_call" | custom-call | tf_op jit(solution)/shard_map/pallas_call | solution.py:471
  80.4 101.4 %shard_map.75 = f32[6144,128]{1,0:T(8,128)S(1)} custom-call(s32[32,8]{1,0:T(8,128)S(1)} %get-tuple-element.18.chosen, f32[8704,128]{1,0:T(8,128)S(1)} %get-tuple-element.19.partial, f32[16384,128]{1,0:T(8,128)} %get-tuple-element.20.extra_hbm, bf16[24576,256]{1,0:T(8,128)(2,1)} %get-tuple-element.14.left_hbm, ...), custom_call_target="tpu_custom_call" | custom-call | tf_op jit(solution)/shard_map/pallas_call | solution.py:672
  181.8 1.7 copy.14
  (8 shorter events, 0.1 us)
Async XLA Ops:
  0.0 0.7 copy-start
  2.8 0.7 copy-start.1

commit v7 on v6

--- a/solution.py
+++ b/solution.py
@@ -359,7 +359,7 @@
 
 def pair_kernel(
     spot_ref, table, left_hbm, right, norm, wcat_hbm, out, extra_hbm, slots,
-    even, even_low, odd, odd_low, left, wcat, extra, near_pairs, far_pairs, near_extra, far_extra, sem,
+    even, even_low, odd, odd_low, left, wcat, extra, near_pairs, far_pairs, near_extra, far_extra, packed, packed_smem, sem,
 ):
     first = pl.ds(0, SPOTS * LEAF)
     later = pl.ds(SPOTS * LEAF, LATER * LEAF)
@@ -378,21 +378,33 @@
 
         lax.fori_loop(0, n, zero, 0)
 
+    spot = spot_ref[0]
+    lane = lax.broadcasted_iota(jnp.int32, (8, 128), 1)
+    lists_here = jnp.full((8, 128), -1, jnp.int32)
+    for n in range(SPOTS):
+        near = pltpu.roll(table[n], (8 * n - 4 * spot + 128) % 128, 1)
+        far = pltpu.roll(table[n], (8 * n + 4 + 64 - 2 * spot) % 128, 1)
+        at = lane - 8 * n
+        lists_here = jnp.where(jnp.logical_and(at >= 0, at < 4), near, lists_here)
+        lists_here = jnp.where(jnp.logical_and(at >= 4, at < 6), far, lists_here)
+    packed[...] = lists_here
+    to_smem = pltpu.make_async_copy(packed, packed_smem, sem.at[4])
+    to_smem.start()
     clear(out, SPOTS + 1)
     clear(extra, LATER + 1)
-    spot = spot_ref[0]
+    to_smem.wait()
 
     def used(t, slot):
-        return table[t % SPOTS, t // SPOTS, slot]
+        return packed_smem[t // SPOTS, 8 * (t % SPOTS) + slot]
 
     def note(t, counts):
         near, far = counts
         for slot in range(4):
-            source = used(t, 4 * spot + slot)
+            source = used(t, slot)
             near_pairs[near] = t * 64 + source
             near = near + jnp.where(source >= 0, 1, 0)
         for slot in range(2):
-            node = used(t, 64 + 2 * spot + slot)
+            node = used(t, 4 + slot)
             far_pairs[far] = t * 64 + node
             far = far + jnp.where(node >= 0, 1, 0)
         return near, far
@@ -401,25 +413,20 @@
 
     def note_later(t, counts):
         near, far = counts
-        slots[t, 0], slots[t, 1] = IDLE // LEAF, 2
+        slots[t, 0] = IDLE // LEAF
         have = 0
         for slot in range(4):
-            source = used(t + SPOTS, 4 * spot + slot)
+            source = used(t + SPOTS, slot)
             hit = source >= 0
             take = jnp.logical_and(hit, have < 1)
             slots[t, jnp.where(take, 0, 7)] = source
             have = have + jnp.where(take, 1, 0)
             near_extra[near] = t * 64 + source
             near = near + jnp.where(jnp.logical_and(hit, jnp.logical_not(take)), 1, 0)
-        have = 0
         for slot in range(2):
-            node = used(t + SPOTS, 64 + 2 * spot + slot)
-            hit = node >= 0
-            take = jnp.logical_and(hit, have < 1)
-            slots[t, jnp.where(take, 1, 7)] = node
-            have = have + jnp.where(take, 1, 0)
+            node = used(t + SPOTS, 4 + slot)
             far_extra[far] = t * 64 + node
-            far = far + jnp.where(jnp.logical_and(hit, jnp.logical_not(take)), 1, 0)
+            far = far + jnp.where(node >= 0, 1, 0)
         return near, far
 
     near_more, far_more = lax.fori_loop(0, LATER, note_later, (0, 0))
@@ -475,7 +482,7 @@
             pltpu.HBM((LATER * LEAF, WCOL), F32),
             jax.ShapeDtypeStruct((LATER, 8), jnp.int32),
         ),
-        in_specs=[smem, smem, hbm, vmem, vmem, hbm],
+        in_specs=[smem, vmem, hbm, vmem, vmem, hbm],
         out_specs=(vmem, hbm, smem),
         scratch_shapes=[VMEM((LEAF, LEAF), BF16)] * 4
         + [
@@ -486,7 +493,9 @@
             pltpu.SMEM((SPOTS * 2 + 3,), jnp.int32),
             pltpu.SMEM((LATER * 4 + 3,), jnp.int32),
             pltpu.SMEM((LATER * 2 + 3,), jnp.int32),
-            pltpu.SemaphoreType.DMA((4,)),
+            VMEM((8, 128), jnp.int32),
+            pltpu.SMEM((8, 128), jnp.int32),
+            pltpu.SemaphoreType.DMA((5,)),
         ],
         compiler_params=pltpu.CompilerParams(vmem_limit_bytes=K2_VMEM),
     )(spot, table, left, right, norm, wcat)
@@ -618,19 +627,19 @@
             if leaf > 0 and n < SIDE:
                 second_axis(k, leaf - 1, j)
 
-    def make(t, slot, width, start_of, high_ref, low_ref):
+    def make(t, high_ref, low_ref):
         at = pl.multiple_of(t * LEAF, LEAF)
-        produce(left, right, norm, at, start_of(chosen[t, slot]), width, high_ref, low_ref)
-
-    def use(t, slot, width, start_of, high_ref, low_ref):
+        produce(left, right, norm, at, near_start(chosen[t, 0]), LEAF, high_ref, low_ref)
+
+    def use(t, high_ref, low_ref):
         at = pl.multiple_of(t * LEAF, LEAF)
-        consume(wcat, sums, at, start_of(chosen[t, slot]), width, high_ref, low_ref)
-
-    def one_target(t):
-        make(t, 1, SKEL, far_start, odd, odd_low)
-        use(t, 0, LEAF, near_start, even, even_low)
-        make((t + 1) % LATER, 0, LEAF, near_start, even, even_low)
-        use(t, 1, SKEL, far_start, odd, odd_low)
+        consume(wcat, sums, at, near_start(chosen[t, 0]), LEAF, high_ref, low_ref)
+
+    def two_targets(t):
+        make(t + 1, odd, odd_low)
+        use(t, even, even_low)
+        make((t + 2) % LATER, even, even_low)
+        use(t + 1, odd, odd_low)
 
     for leaf in range(MINE + 1):
         if leaf < MINE:
@@ -638,15 +647,11 @@
         if leaf == 0:
             for c in loads:
                 c.wait()
-            make(0, 0, LEAF, near_start, even, even_low)
+            make(0, even, even_low)
         if leaf < MINE - 1:
 
             def step(n, _, leaf=leaf):
-                def inner(m, carry):
-                    one_target(leaf * SPOTS + 2 * n + m)
-                    return carry
-
-                lax.fori_loop(0, 2, inner, 0)
+                two_targets(leaf * SPOTS + 2 * n)
                 for which in range(2 * SIDE):
                     pl.when(n == which)(functools.partial(part, leaf, which))
                 return _
@@ -681,8 +686,7 @@
             VMEM((LATER * LEAF, 256), BF16),
             VMEM((BLOCKS, BLOCK, 2 * WCOL), BF16),
         ]
-        + [VMEM((LEAF, LEAF), BF16)] * 2
-        + [VMEM((LEAF, SKEL), BF16)] * 2
+        + [VMEM((LEAF, LEAF), BF16)] * 4
         + [
             pltpu.SemaphoreType.DMA((4, MINE * 3 * SIDE)),
             pltpu.SemaphoreType.DMA((4, MINE * 3 * SIDE)),

time: 184 us -> 182 us (0.989)
  Pallas kernels: 178 us -> 176 us
where the time goes in v7:
time: 182 us; the launch traced here: 181 us
  Pallas kernels  176 us (97%)
  local copies, waits for them, and re-layouts  4.66 us (3%)
    pallas_call x1, Pallas kernels, scatter(): pl.pallas_call(scatter_kernel, out_shape=jax.ShapeDtypeStruct((COLPTS, WC...  99.9 us
    pallas_call x1, Pallas kernels, gather(): pl.pallas_call(gather_kernel, out_shape=(pltpu.HBM((TARGETS * LEAF, 256),...  51.9 us
    pallas_call x1, Pallas kernels, pairs(): pl.pallas_call(pair_kernel, out_shape=(pltpu.VMEM(((SPOTS + 1) * LEAF, WC...  24.4 us
    unnamed x6, local copies, waits for them, and re-layouts  3.71 us

profile of v7, /device:TPU:0, one launch (start us, length us, event | category | flops | bytes accessed | tf_op | source)
XLA Modules:
  0.0 181.4 jit_solution(14455413110790360990)
XLA Ops:
  0.0 0.0 copy-start
  0.0 0.1 iota_compare_fusion.2
  0.1 0.6 copy-done
  0.7 0.1 fusion
  0.8 0.8 constant_dynamic-slice_fusion
  1.6 0.1 copy.12
  1.6 0.1 fusion.1
  1.7 0.8 copy.11
  2.5 0.1 broadcast_in_dim.43
  2.6 0.1 select_reduce_fusion
  2.7 0.1 pad_add_fusion
  2.8 0.0 copy-start.1
  2.8 0.7 copy-done.1
  3.5 51.9 %shard_map.73 = (bf16[24576,256]{1,0:T(8,128)(2,1)}, bf16[52,256,256]{2,1,0:T(8,128)(2,1)S(1)}, f32[52,1,256]{2,1,0:T(1,128)S(1)}, bf16[52,256,256]{2,1,0:T(8,128)(2,1)}, s32[16,8,128]{2,1,0:T(8,128)S(1)}) custom-call(f32[64,6144]{1,0:T(8,128)} %points_hbm.1, f32[6144,128]{1,0:T(8,128)} %weights_hbm.1, f32[256,6144]{1,0:T(8,128)} %proj_hbm.1, ...), custom_call_target="tpu_custom_call" | custom-call | tf_op jit(solution)/shard_map/pallas_call | solution.py:298
  55.4 24.4 %shard_map.74 = (f32[8704,128]{1,0:T(8,128)S(1)}, f32[16384,128]{1,0:T(8,128)}, s32[32,8]{1,0:T(8,128)S(1)}) custom-call(s32[1]{0:T(128)} %bitcast.spot_ref, s32[16,8,128]{2,1,0:T(8,128)S(1)} %get-tuple-element.13.table, bf16[24576,256]{1,0:T(8,128)(2,1)} %get-tuple-element.14.left_hbm, bf16[52,256,256]{2,1,0:T(8,128)(2,1)S(1)} %get-tuple-element.15.right, ...), custom_call_target="tpu_custom_call" | custom-call | tf_op jit(solution)/shard_map/pallas_call | solution.py:478
  79.8 99.9 %shard_map.75 = f32[6144,128]{1,0:T(8,128)S(1)} custom-call(s32[32,8]{1,0:T(8,128)S(1)} %get-tuple-element.18.chosen, f32[8704,128]{1,0:T(8,128)S(1)} %get-tuple-element.19.partial, f32[16384,128]{1,0:T(8,128)} %get-tuple-element.20.extra_hbm, bf16[24576,256]{1,0:T(8,128)(2,1)} %get-tuple-element.14.left_hbm, ...), custom_call_target="tpu_custom_call" | custom-call | tf_op jit(solution)/shard_map/pallas_call | solution.py:677
  179.7 1.7 copy.14
  (8 shorter events, 0.1 us)
Async XLA Ops:
  0.0 0.7 copy-start
  2.8 0.7 copy-start.1

commit v8 on v7

--- a/solution.py
+++ b/solution.py
@@ -644,15 +644,19 @@
     for leaf in range(MINE + 1):
         if leaf < MINE:
             start_leaf(leaf)
+        begun = 0
         if leaf == 0:
+            begun = 2
+            for n in range(begun):
+                part(leaf, n)
             for c in loads:
                 c.wait()
             make(0, even, even_low)
         if leaf < MINE - 1:
 
-            def step(n, _, leaf=leaf):
+            def step(n, _, leaf=leaf, begun=begun):
                 two_targets(leaf * SPOTS + 2 * n)
-                for which in range(2 * SIDE):
+                for which in range(begun, 2 * SIDE):
                     pl.when(n == which)(functools.partial(part, leaf, which))
                 return _
 

time: 182 us -> 183 us (level)
    pallas_call x1, Pallas kernels: 24.4 us -> 36.2 us  [pairs(): pl.pallas_call(pair_kernel, out_shape=(pltpu.VMEM(((SPOTS + 1) * LEAF, WC...]
    pallas_call x1, Pallas kernels: 99.9 us -> 89.2 us  [scatter(): pl.pallas_call(scatter_kernel, out_shape=jax.ShapeDtypeStruct((COLPTS, WC...]
where the time goes in v8:
time: 183 us; the launch traced here: 182 us
  Pallas kernels  177 us (97%)
  local copies, waits for them, and re-layouts  4.66 us (3%)
    pallas_call x1, Pallas kernels, scatter(): pl.pallas_call(scatter_kernel, out_shape=jax.ShapeDtypeStruct((COLPTS, WC...  89.2 us
    pallas_call x1, Pallas kernels, gather(): pl.pallas_call(gather_kernel, out_shape=(pltpu.HBM((TARGETS * LEAF, 256),...  51.9 us
    pallas_call x1, Pallas kernels, pairs(): pl.pallas_call(pair_kernel, out_shape=(pltpu.VMEM(((SPOTS + 1) * LEAF, WC...  36.2 us
    unnamed x6, local copies, waits for them, and re-layouts  3.71 us

profile of v8, /device:TPU:0, one launch (start us, length us, event | category | flops | bytes accessed | tf_op | source)
XLA Modules:
  0.0 182.4 jit_solution(17670795102764246991)
XLA Ops:
  0.0 0.0 copy-start
  0.0 0.1 iota_compare_fusion.2
  0.1 0.6 copy-done
  0.7 0.1 fusion
  0.8 0.8 constant_dynamic-slice_fusion
  1.6 0.1 copy.12
  1.6 0.1 fusion.1
  1.7 0.8 copy.11
  2.5 0.1 broadcast_in_dim.43
  2.6 0.1 select_reduce_fusion
  2.7 0.1 pad_add_fusion
  2.8 0.0 copy-start.1
  2.8 0.7 copy-done.1
  3.5 51.9 %shard_map.73 = (bf16[24576,256]{1,0:T(8,128)(2,1)}, bf16[52,256,256]{2,1,0:T(8,128)(2,1)S(1)}, f32[52,1,256]{2,1,0:T(1,128)S(1)}, bf16[52,256,256]{2,1,0:T(8,128)(2,1)}, s32[16,8,128]{2,1,0:T(8,128)S(1)}) custom-call(f32[64,6144]{1,0:T(8,128)} %points_hbm.1, f32[6144,128]{1,0:T(8,128)} %weights_hbm.1, f32[256,6144]{1,0:T(8,128)} %proj_hbm.1, ...), custom_call_target="tpu_custom_call" | custom-call | tf_op jit(solution)/shard_map/pallas_call | solution.py:298
  55.4 36.2 %shard_map.74 = (f32[8704,128]{1,0:T(8,128)S(1)}, f32[16384,128]{1,0:T(8,128)}, s32[32,8]{1,0:T(8,128)S(1)}) custom-call(s32[1]{0:T(128)} %bitcast.spot_ref, s32[16,8,128]{2,1,0:T(8,128)S(1)} %get-tuple-element.13.table, bf16[24576,256]{1,0:T(8,128)(2,1)} %get-tuple-element.14.left_hbm, bf16[52,256,256]{2,1,0:T(8,128)(2,1)S(1)} %get-tuple-element.15.right, ...), custom_call_target="tpu_custom_call" | custom-call | tf_op jit(solution)/shard_map/pallas_call | solution.py:478
  91.6 89.2 %shard_map.75 = f32[6144,128]{1,0:T(8,128)S(1)} custom-call(s32[32,8]{1,0:T(8,128)S(1)} %get-tuple-element.18.chosen, f32[8704,128]{1,0:T(8,128)S(1)} %get-tuple-element.19.partial, f32[16384,128]{1,0:T(8,128)} %get-tuple-element.20.extra_hbm, bf16[24576,256]{1,0:T(8,128)(2,1)} %get-tuple-element.14.left_hbm, ...), custom_call_target="tpu_custom_call" | custom-call | tf_op jit(solution)/shard_map/pallas_call | solution.py:681
  180.8 1.7 copy.14
  (8 shorter events, 0.1 us)
Async XLA Ops:
  0.0 0.7 copy-start
  2.8 0.7 copy-start.1

commit v9 on v7

--- a/solution.py
+++ b/solution.py
@@ -263,10 +263,11 @@
         coords[...] += mm(first, pick) + mm(second, pick) + mm(third, pick)
         return _
 
-    lax.fori_loop(0, COLPTS // CHUNK, skeleton, 0)
+    lax.fori_loop(0, COLPTS // CHUNK // 2, skeleton, 0)
+    forward(2)
+    lax.fori_loop(COLPTS // CHUNK // 2, COLPTS // CHUNK, skeleton, 0)
     swap(2, coords, coords2)
     swap(3, values, values2)
-    forward(2)
     put_source(coords[...], right, norm, 2 * COLPTS // BLOCK)
     put_weights(values[...], wcat, 2 * COLPTS // BLOCK)
     swaps[0].wait_recv()

time: 182 us -> 182 us (level)
  no operation moved by 1% of the time
where the time goes in v9:
time: 182 us; the launch traced here: 181 us
  Pallas kernels  176 us (97%)
  local copies, waits for them, and re-layouts  4.66 us (3%)
    pallas_call x1, Pallas kernels, scatter(): pl.pallas_call(scatter_kernel, out_shape=jax.ShapeDtypeStruct((COLPTS, WC...  98.7 us
    pallas_call x1, Pallas kernels, gather(): pl.pallas_call(gather_kernel, out_shape=(pltpu.HBM((TARGETS * LEAF, 256),...  51.2 us
    pallas_call x1, Pallas kernels, pairs(): pl.pallas_call(pair_kernel, out_shape=(pltpu.VMEM(((SPOTS + 1) * LEAF, WC...  25.8 us
    unnamed x6, local copies, waits for them, and re-layouts  3.71 us

profile of v9, /device:TPU:0, one launch (start us, length us, event | category | flops | bytes accessed | tf_op | source)
XLA Modules:
  0.0 180.9 jit_solution(13436575874600961911)
XLA Ops:
  0.0 0.0 copy-start
  0.0 0.1 iota_compare_fusion.2
  0.1 0.6 copy-done
  0.7 0.1 fusion
  0.8 0.8 constant_dynamic-slice_fusion
  1.6 0.1 copy.12
  1.6 0.1 fusion.1
  1.7 0.8 copy.11
  2.5 0.1 broadcast_in_dim.43
  2.6 0.1 select_reduce_fusion
  2.7 0.1 pad_add_fusion
  2.8 0.0 copy-start.1
  2.8 0.7 copy-done.1
  3.5 51.2 %shard_map.73 = (bf16[24576,256]{1,0:T(8,128)(2,1)}, bf16[52,256,256]{2,1,0:T(8,128)(2,1)S(1)}, f32[52,1,256]{2,1,0:T(1,128)S(1)}, bf16[52,256,256]{2,1,0:T(8,128)(2,1)}, s32[16,8,128]{2,1,0:T(8,128)S(1)}) custom-call(f32[64,6144]{1,0:T(8,128)} %points_hbm.1, f32[6144,128]{1,0:T(8,128)} %weights_hbm.1, f32[256,6144]{1,0:T(8,128)} %proj_hbm.1, ...), custom_call_target="tpu_custom_call" | custom-call | tf_op jit(solution)/shard_map/pallas_call | solution.py:299
  54.7 25.8 %shard_map.74 = (f32[8704,128]{1,0:T(8,128)S(1)}, f32[16384,128]{1,0:T(8,128)}, s32[32,8]{1,0:T(8,128)S(1)}) custom-call(s32[1]{0:T(128)} %bitcast.spot_ref, s32[16,8,128]{2,1,0:T(8,128)S(1)} %get-tuple-element.13.table, bf16[24576,256]{1,0:T(8,128)(2,1)} %get-tuple-element.14.left_hbm, bf16[52,256,256]{2,1,0:T(8,128)(2,1)S(1)} %get-tuple-element.15.right, ...), custom_call_target="tpu_custom_call" | custom-call | tf_op jit(solution)/shard_map/pallas_call | solution.py:479
  80.5 98.7 %shard_map.75 = f32[6144,128]{1,0:T(8,128)S(1)} custom-call(s32[32,8]{1,0:T(8,128)S(1)} %get-tuple-element.18.chosen, f32[8704,128]{1,0:T(8,128)S(1)} %get-tuple-element.19.partial, f32[16384,128]{1,0:T(8,128)} %get-tuple-element.20.extra_hbm, bf16[24576,256]{1,0:T(8,128)(2,1)} %get-tuple-element.14.left_hbm, ...), custom_call_target="tpu_custom_call" | custom-call | tf_op jit(solution)/shard_map/pallas_call | solution.py:678
  179.2 1.7 copy.14
  (8 shorter events, 0.1 us)
Async XLA Ops:
  0.0 0.7 copy-start
  2.8 0.7 copy-start.1
